TPU v7x, 128 devices: a whole 4x4x4 slice. The times are simulated.
128 devices in a mesh: resp: 16 (over z, x_hi, core), tp: 8 (over x_lo, y).
Axes of the slice: x: 4 (x_hi: 2, x_lo: 2; x = x_hi * 2 + x_lo), y: 4, z: 4, core: 2. Of those that a mesh axis runs over, the one named last changes fastest.
Arguments:
- queries: bfloat16 [16, 512, 5120], P('resp', None, 'tp'), may hold values from -5 to 5
- response_keys: bfloat16 [16, 512, 1024], P('resp', None, 'tp'), may hold values from -5 to 5
- response_values: bfloat16 [16, 512, 1024], P('resp', None, 'tp'), may hold values from -5 to 5
- prompt_key_rows: bfloat16 [1024, 1024], P('resp', 'tp'), may hold values from -5 to 5
- prompt_value_rows: bfloat16 [1024, 1024], P('resp', 'tp'), may hold values from -5 to 5
- upstream: bfloat16 [16, 512, 5120], P('resp', 'tp'), may hold values from -6 to 6
- lengths: int32 [16], P('resp'), may hold values from 128 to 512, as said below
- query_weight: bfloat16 [5120, 5120], P(None, 'tp'), may hold values from -0.078125 to 0.078125
- key_matrix: bfloat16 [5120, 1024], P(None, 'tp'), may hold values from -0.078125 to 0.078125
- value_matrix: bfloat16 [5120, 1024], P(None, 'tp'), may hold values from -0.078125 to 0.078125
- out_weight: bfloat16 [5120, 5120], P('tp'), may hold values from -2.5 to 2.5
Outputs:
- input_grad: bfloat16 [16, 512, 5120], P('resp', 'tp')
- prompt_key_gradient: float32 [1024, 1024], P('resp', 'tp')
- prompt_value_gradient: float32 [1024, 1024], P('resp', 'tp')
Inputs may be any that keep to these rules, and one draw needn't show every extreme that they name: `lengths`: one response of each draw has exactly 512 live tokens.
All inputs are finite; a program needn't handle non-finite values.
Results may differ from a plain program's by a relative error of at most 0.018.
Values may be sent and summed in bfloat16 or wider, within the bound.
A program may use at most 128 MiB of HBM per device.

v0:
```python
import math

import jax
import jax.numpy as jnp
from jax import lax
from jax.sharding import PartitionSpec as P

HEAD_WIDTH = 128


def head_backward(query_head, grad_head, head_of_keys, value_head, scaling):
    row_total = query_head.shape[0]
    key_total = head_of_keys.shape[0]
    prompt_len = key_total - row_total
    scores = (
        lax.dot_general(
            query_head, head_of_keys, (((1,), (1,)), ((), ())), preferred_element_type=jnp.float32
        )
        * scaling
    )
    positions = jnp.arange(row_total, dtype=jnp.int32)[:, None]
    key_index = jnp.arange(key_total, dtype=jnp.int32)[None, :]
    visible = (key_index < prompt_len) | (key_index - prompt_len <= positions)
    scores = jnp.where(visible, scores, -jnp.inf)
    row_max = jnp.max(scores, axis=1, keepdims=True)
    exponent = jnp.exp(scores - row_max)
    probability = exponent / jnp.sum(exponent, axis=1, keepdims=True)
    probability_b = probability.astype(jnp.bfloat16)
    grad_prob = lax.dot_general(
        grad_head, value_head, (((1,), (1,)), ((), ())), preferred_element_type=jnp.float32
    )
    row_delta = jnp.sum(probability * grad_prob, axis=1, keepdims=True)
    grad_score = (probability * (grad_prob - row_delta) * scaling).astype(jnp.bfloat16)
    query_gradient = jnp.dot(grad_score, head_of_keys, preferred_element_type=jnp.float32).astype(
        jnp.bfloat16
    )
    key_term = lax.dot_general(
        grad_score, query_head, (((0,), (0,)), ((), ())), preferred_element_type=jnp.float32
    )
    value_term = lax.dot_general(
        probability_b, grad_head, (((0,), (0,)), ((), ())), preferred_element_type=jnp.float32
    )
    return (query_gradient, key_term, value_term)


def body(
    queries,
    response_keys,
    response_values,
    prompt_key_rows,
    prompt_value_rows,
    upstream,
    lengths,
    query_weight,
    key_matrix,
    value_matrix,
    out_weight,
):
    scaling = 1.0 / math.sqrt(HEAD_WIDTH)
    resp_len = queries.shape[1]
    heads_local = queries.shape[2] // HEAD_WIDTH
    kvheads_local = response_keys.shape[2] // HEAD_WIDTH
    sample_count = heads_local // kvheads_local
    live_len = lengths[0]
    piece_rows = lax.all_gather(upstream, "tp", axis=1, tiled=True)
    positions = jnp.arange(piece_rows.shape[1], dtype=jnp.int32)
    masked = jnp.where(
        (positions < live_len)[None, :, None], piece_rows, jnp.zeros((), piece_rows.dtype)
    )
    projected = lax.dot_general(
        masked[0], out_weight, (((1,), (1,)), ((), ())), preferred_element_type=jnp.float32
    )
    grad_out = projected.astype(jnp.bfloat16)[None]
    shared_keys, shared_values = (
        lax.all_gather(prompt_key_rows, "resp", axis=0, tiled=True),
        lax.all_gather(prompt_value_rows, "resp", axis=0, tiled=True),
    )
    prompt_len = shared_keys.shape[0]
    every_key = jnp.concatenate(
        [
            shared_keys.reshape(prompt_len, kvheads_local, HEAD_WIDTH),
            response_keys[0].reshape(resp_len, kvheads_local, HEAD_WIDTH),
        ],
        axis=0,
    )
    every_value = jnp.concatenate(
        [
            shared_values.reshape(prompt_len, kvheads_local, HEAD_WIDTH),
            response_values[0].reshape(resp_len, kvheads_local, HEAD_WIDTH),
        ],
        axis=0,
    )
    query_heads = queries[0].reshape(resp_len, heads_local, HEAD_WIDTH)
    grad_heads = grad_out[0].reshape(resp_len, heads_local, HEAD_WIDTH)

    def head_step(carried, head_index):
        key_sums, value_sums = carried
        pair_index = head_index // sample_count
        query_head = lax.dynamic_index_in_dim(query_heads, head_index, 1, keepdims=False)
        grad_head = lax.dynamic_index_in_dim(grad_heads, head_index, 1, keepdims=False)
        head_of_keys = lax.dynamic_index_in_dim(every_key, pair_index, 1, keepdims=False)
        value_head = lax.dynamic_index_in_dim(every_value, pair_index, 1, keepdims=False)
        query_gradient, key_term, value_term = head_backward(
            query_head, grad_head, head_of_keys, value_head, scaling
        )
        old_key = lax.dynamic_index_in_dim(key_sums, pair_index, 1, keepdims=False)
        old_value = lax.dynamic_index_in_dim(value_sums, pair_index, 1, keepdims=False)
        key_sums = lax.dynamic_update_index_in_dim(key_sums, old_key + key_term, pair_index, 1)
        value_sums = lax.dynamic_update_index_in_dim(
            value_sums, old_value + value_term, pair_index, 1
        )
        return ((key_sums, value_sums), query_gradient)

    zero_sums = jnp.zeros((prompt_len + resp_len, kvheads_local, HEAD_WIDTH), jnp.float32)
    (key_sums, value_sums), grad_queries = lax.scan(
        head_step, (zero_sums, zero_sums), jnp.arange(heads_local, dtype=jnp.int32)
    )
    grad_flat = grad_queries.transpose(1, 0, 2).reshape(resp_len, heads_local * HEAD_WIDTH)
    response_key_gradient = (
        key_sums[prompt_len:].astype(jnp.bfloat16).reshape(resp_len, kvheads_local * HEAD_WIDTH)
    )
    response_value_gradient = (
        value_sums[prompt_len:].astype(jnp.bfloat16).reshape(resp_len, kvheads_local * HEAD_WIDTH)
    )
    prompt_key_part = key_sums[:prompt_len].reshape(prompt_len, kvheads_local * HEAD_WIDTH)
    prompt_value_part = value_sums[:prompt_len].reshape(prompt_len, kvheads_local * HEAD_WIDTH)
    contract_cols = (((1,), (1,)), ((), ()))
    term = lax.dot_general(
        grad_flat, query_weight, contract_cols, preferred_element_type=jnp.float32
    )
    term = term + lax.dot_general(
        response_key_gradient, key_matrix, contract_cols, preferred_element_type=jnp.float32
    )
    term = term + lax.dot_general(
        response_value_gradient, value_matrix, contract_cols, preferred_element_type=jnp.float32
    )
    summed = lax.psum_scatter(term.astype(jnp.bfloat16), "tp", scatter_dimension=0, tiled=True)
    prompt_key_gradient, prompt_value_gradient = (
        lax.psum_scatter(
            prompt_key_part.astype(jnp.bfloat16), "resp", scatter_dimension=0, tiled=True
        ).astype(jnp.float32),
        lax.psum_scatter(
            prompt_value_part.astype(jnp.bfloat16), "resp", scatter_dimension=0, tiled=True
        ).astype(jnp.float32),
    )
    input_grad = summed[None]
    return (input_grad, prompt_key_gradient, prompt_value_gradient)


def solution(mesh):
    in_specs = (
        P("resp", None, "tp"),
        P("resp", None, "tp"),
        P("resp", None, "tp"),
        P("resp", "tp"),
        P("resp", "tp"),
        P("resp", "tp", None),
        P("resp"),
        P(None, "tp"),
        P(None, "tp"),
        P(None, "tp"),
        P("tp", None),
    )
    out_specs = (P("resp", "tp", None), P("resp", "tp"), P("resp", "tp"))
    return jax.shard_map(body, mesh=mesh, in_specs=in_specs, out_specs=out_specs, check_vma=False)
```

profile of v0, /device:TPU:1, one launch (start us, length us, event | category | flops | bytes accessed | tf_op | source)
XLA Modules:
  0.0 358.5 jit_solution(8923250348972661946)
XLA Ops:
  8.6 2.2 copy.14
  10.8 29.2 %all_gather.9 = bf16[1024,128]{1,0:T(8,128)(2,1)S(1)} all-gather(bf16[64,128]{1,0:T(8,128)(2,1)} %param.16), channel_id=1, replica_groups=mesh['resp'=16,'tp'=8] {'resp'}, dimensions={0}, use_global_device_ids=true | all-gather | bytes 278528 | tf_op jit(solution)/shard_map/all_gather | solution.py:75
  40.0 22.4 %all_gather.11 = bf16[1024,128]{1,0:T(8,128)(2,1)S(1)} all-gather(bf16[64,128]{1,0:T(8,128)(2,1)} %param.17), channel_id=1, replica_groups=mesh['resp'=16,'tp'=8] {'resp'}, dimensions={0}, use_global_device_ids=true | all-gather | bytes 278528 | tf_op jit(solution)/shard_map/all_gather | solution.py:76
  64.1 15.1 %all-gather.2.cloned.1.call-done = bf16[1,512,5120]{2,1,0:T(8,128)(2,1)} async-done(((bf16[1,64,5120]{2,1,0:T(8,128)(2,1)}), bf16[1,512,5120]{2,1,0:T(8,128)(2,1)}) %all-gather.2.cloned.1.call-update) | async-done | bytes 5242896 | tf_op jit(solution)/shard_map/all_gather | solution.py:65
  79.2 8.7 %fusion.30 = bf16[512,640]{1,0:T(8,128)(2,1)S(1)} fusion(bf16[640,5120]{1,0:T(8,128)(2,1)} %param.23, bf16[1,512,5120]{2,1,0:T(8,128)(2,1)} %all-gather.2.cloned.1.call-done, pred[512]{0:T(512)(128)(4,1)S(1)} %iota_compare_fusion.2), kind=kOutput, calls=%fused_computation.41 | convolution fusion | flops 3358392320 | bytes 12452352 | tf_op jit(solution)/shard_map/dot_general | solution.py:70
  89.1 65.5 %while.16 = (s32[]{:T(128)}, f32[1536,1,128]{2,0,1:T(8,128)S(1)}, f32[1536,1,128]{2,0,1:T(8,128)S(1)}, bf16[5,512,128]{1,2,0:T(8,128)(2,1)}, s32[5]{0:T(128)S(1)...) while((s32[]{:T(128)}, f32[1536,1,128]{2,0,1:T(8,128)S(1)}, ...), condition=%wide.region_4.5_spmd, body=%wide.region_0.4_spmd.sunk | while | flops 1022821888 | bytes 33854684 | solution.py:115
  91.7 2.0 fusion.61
  94.3 2.1 fusion.64
  96.3 2.0 multiply_reduce_fusion.2
  104.8 2.0 fusion.61
  107.4 2.1 fusion.64
  109.5 2.0 multiply_reduce_fusion.2
  117.9 2.0 fusion.61
  120.5 2.1 fusion.64
  131.0 2.0 fusion.61
  133.6 2.1 fusion.64
  144.1 2.0 fusion.61
  146.7 2.1 fusion.64
  156.3 5.4 %fusion.33 = f32[512,5120]{1,0:T(8,128)} fusion(bf16[5120,128]{1,0:T(8,128)(2,1)S(1)} %copy-done, bf16[1536,1,128]{2,0,1:T(8,128)(2,1)S(1)} %convert.8), kind=kOutput, calls=%fused_computation.48 | convolution fusion | flops 671088640 | bytes 11927552 | tf_op jit(solution)/shard_map/dot_general | solution.py:131
  161.9 10.0 %fusion.36 = f32[512,5120]{1,0:T(8,128)} fusion(bf16[512,640]{0,1:T(8,128)(2,1)S(1)} %bitcast.112, bf16[5120,640]{1,0:T(8,128)(2,1)} %param.20), kind=kOutput, calls=%fused_computation.52 | convolution fusion | flops 3355443200 | bytes 17694720 | tf_op jit(solution)/shard_map/dot_general | solution.py:128
  171.9 8.3 %add_convert_fusion = bf16[512,5120]{1,0:T(8,128)(2,1)} fusion(f32[512,5120]{1,0:T(8,128)} %fusion.36, f32[512,5120]{1,0:T(8,128)S(1)} %copy-done.1, bf16[5120,128]{1,0:T(8,128)(2,1)S(1)} %copy-done.2, bf16[1536,1,128]{2,0,1:T(8,128)(2,1)S(1)} %convert.9), kind=kOutput, calls=%fused_computation.35 | convolution fusion | flops 678952960 | bytes 27656192 | tf_op jit(solution)/shard_map/dot_general | solution.py:134
  180.2 37.2 %reduce-scatter.6.cloned.1.call-done = bf16[64,128]{1,0:T(8,128)(2,1)} async-done(((bf16[1024,128]{1,0:T(8,128)(2,1)}), bf16[64,128]{1,0:T(8,128)(2,1)}) %reduce-scatter.6.cloned.1.call-update) | async-done | bytes 16400 | tf_op jit(solution)/shard_map/reduce_scatter | solution.py:139
  218.7 66.6 %reduce-scatter.8.cloned.1.call-done = bf16[64,128]{1,0:T(8,128)(2,1)} async-done(((bf16[1024,128]{1,0:T(8,128)(2,1)}), bf16[64,128]{1,0:T(8,128)(2,1)}) %reduce-scatter.8.cloned.1.call-update) | async-done | bytes 16400 | tf_op jit(solution)/shard_map/reduce_scatter | solution.py:142
  286.6 65.4 %reduce-scatter.4.cloned.1.call-done = bf16[64,5120]{1,0:T(8,128)(2,1)} async-done(((bf16[512,5120]{1,0:T(8,128)(2,1)}), bf16[64,5120]{1,0:T(8,128)(2,1)}) %reduce-scatter.4.cloned.1.call-update) | async-done | bytes 655376 | tf_op jit(solution)/shard_map/reduce_scatter | solution.py:137
  (90 shorter events, 39.4 us)
Async XLA Ops:
  7.2 149.1 %copy-start = (bf16[5120,128]{1,0:T(8,128)(2,1)S(1)}, bf16[5120,128]{1,0:T(8,128)(2,1)}, u32[]{:S(2)}) copy-start(bf16[5120,128]{1,0:T(8,128)(2,1)} %param.21) | copy-start | bytes 3932164
  7.2 56.1 %copy-start.4 = (bf16[1,512,128]{2,1,0:T(8,128)(2,1)S(1)}, bf16[1,512,128]{2,1,0:T(8,128)(2,1)}, u32[]{:S(2)}) copy-start(bf16[1,512,128]{2,1,0:T(8,128)(2,1)} %param.15) | copy-start | bytes 393220
  7.2 72.0 %all-gather.2.cloned.1.call-start = ((), (), s32[]{:S(2)}) async-start(), calls=%async_computation.3 | async-start | bytes 5898240 | tf_op jit(solution)/shard_map/all_gather | solution.py:65
  7.9 209.4 %reduce-scatter.6.cloned.1.call-start = ((), (), s32[]{:S(2)}) async-start(), calls=%async_computation.5 | async-start | bytes 278528 | tf_op jit(solution)/shard_map/reduce_scatter | solution.py:139
  94.3 2.1 copy-start.3
  107.4 2.1 copy-start.3
  120.5 2.1 copy-start.3
  133.6 2.1 copy-start.3
  146.7 2.1 copy-start.3
  155.4 129.8 %reduce-scatter.8.cloned.1.call-start = ((), (), s32[]{:S(2)}) async-start(), calls=%async_computation.6 | async-start | bytes 278528 | tf_op jit(solution)/shard_map/reduce_scatter | solution.py:142
  156.3 5.6 %copy-start.5 = (bf16[5,512,128]{1,2,0:T(8,128)(2,1)S(1)}, bf16[5,512,128]{1,2,0:T(8,128)(2,1)}, u32[]{:S(2)}) copy-start(bf16[5,512,128]{1,2,0:T(8,128)(2,1)} %get-tuple-element.118) | copy-start | bytes 1966084
  161.6 190.3 %reduce-scatter.4.cloned.1.call-start = ((), (), s32[]{:S(2)}) async-start(), calls=%async_computation.4 | async-start | bytes 5898240 | tf_op jit(solution)/shard_map/reduce_scatter | solution.py:137
  161.9 10.0 %copy-start.1 = (f32[512,5120]{1,0:T(8,128)S(1)}, f32[512,5120]{1,0:T(8,128)}, u32[]{:S(2)}) copy-start(f32[512,5120]{1,0:T(8,128)} %fusion.33) | copy-start | bytes 31457284
  161.9 10.0 %copy-start.2 = (bf16[5120,128]{1,0:T(8,128)(2,1)S(1)}, bf16[5120,128]{1,0:T(8,128)(2,1)}, u32[]{:S(2)}) copy-start(bf16[5120,128]{1,0:T(8,128)(2,1)} %param.22) | copy-start | bytes 3932164
Sparse Core Ops, SparseCore 0:
  9.7 69.4 all-gather.1
  155.5 61.7 reduce-scatter.5
  221.0 64.1 reduce-scatter.7
  288.1 63.8 reduce-scatter.3
where the time goes:
time: 359 us
  waiting for transfers between devices  185 us (52%)
  matrix products  73.5 us (20%)
  blocking collectives  51.5 us (14%)
  between operations  14.5 us (4%)
  other arithmetic  11.9 us (3%)
  local copies, waits for them, and re-layouts  11.7 us (3%)
  loops' own time  10 us (3%)
    reduce_scatter x1, waiting for transfers between devices, body(): lax.psum_scatter(prompt_value_part.astype(jnp.bfloat16), 'resp', scatter_...  66.6 us
    reduce_scatter x1, waiting for transfers between devices, body(): lax.psum_scatter(term.astype(jnp.bfloat16), 'tp', scatter_dimension=0, ti...  65.4 us
    reduce_scatter x1, waiting for transfers between devices, body(): lax.psum_scatter(prompt_key_part.astype(jnp.bfloat16), 'resp', scatter_di...  37.2 us
    all_gather x1, blocking collectives, body(): lax.all_gather(prompt_key_rows, 'resp', axis=0, tiled=True)  29.2 us
    all_gather x1, blocking collectives, body(): lax.all_gather(prompt_value_rows, 'resp', axis=0, tiled=True)  22.4 us
    all_gather x1, waiting for transfers between devices, body(): piece_rows = lax.all_gather(upstream, 'tp', axis=1, tiled=True)  15.1 us
    dot_general x5, matrix products, head_backward(): lax.dot_general(probability_b, grad_head, (((0,), (0,)), ((), ())), prefe...  10.3 us
    another operation x1, loops' own time, body(): lax.scan(head_step, (zero_sums, zero_sums), jnp.arange(heads_local, dtype...  10 us
  transfers between devices with their start and end apart: 4, of which 4 were waited for; matrix products, arithmetic and copies ran while one was open for 9% of the time, Pallas kernels for 0%

commit v1 on v0

v1 whole, which is shorter than its diff:
```python
import functools
import math

import jax
import jax.numpy as jnp
from jax import lax
from jax.experimental import pallas as pl
from jax.experimental.pallas import tpu as pltpu
from jax.sharding import PartitionSpec as P

MESH = pl.DeviceIdType.MESH
BF = jnp.bfloat16
F32 = jnp.float32
WIDTH = 5120
HEADS = 5
HEAD = 128
ROWS = 64
GROUP = 256
CHUNK = 256
LANES = HEADS * GROUP
HALF = WIDTH // 2
QUARTER = WIDTH // 4
NT = (((1,), (1,)), ((), ()))


def dot_nt(a, b):
    return lax.dot_general(a, b, NT, preferred_element_type=F32)


def dot(a, b):
    return jnp.dot(a, b, preferred_element_type=F32)


def kernel(
    len_ref,
    q_hbm,
    rk_hbm,
    rv_hbm,
    pk_hbm,
    pv_hbm,
    up_ref,
    wq_hbm,
    wk_hbm,
    wv_hbm,
    wo_hbm,
    out_ref,
    pkg_ref,
    pvg_ref,
    blocks,
    wo,
    wc,
    q,
    kv,
    kt,
    vt,
    scores,
    prob,
    out_t,
    go_acc,
    go,
    delta,
    ds,
    dq_t,
    dkv,
    grads,
    landed,
    p_send,
    p_land,
    p_land_z,
    p_land_h,
    load_sem,
    gs_sem,
    gr_sem,
    rs_sem,
    rr_sem,
    ps_sem,
    pr_sem,
):
    r = lax.axis_index("resp")
    t = lax.axis_index("tp")
    z, xh, core = r // 4, (r // 2) % 2, r % 2
    xl, y = t // 4, t % 4
    up1, down1, far1 = (y + 1) % 4, (y + 3) % 4, (y + 2) % 4
    ox = 1 - xl
    i_x, i_u, i_d, i_f = ox * 4 + y, xl * 4 + up1, xl * 4 + down1, xl * 4 + far1
    i_xu, i_xd, i_xf = ox * 4 + up1, ox * 4 + down1, ox * 4 + far1
    dev_x, dev_u, dev_d = (r, i_x), (r, i_u), (r, i_d)
    dev_s = (z * 4 + xh * 2 + 1 - core, t)
    dev_h = (z * 4 + (1 - xh) * 2 + core, t)
    dev_z = [(((z + k) % 4) * 4 + xh * 2 + core, t) for k in (1, 2, 3)]

    barrier = pltpu.get_barrier_semaphore()
    peers = [dev_x, dev_u, dev_d, dev_s, dev_h] + dev_z
    for peer in peers:
        pl.semaphore_signal(barrier, inc=1, device_id=peer, device_id_type=MESH)

    loads = []

    def load(src, dst):
        copy = pltpu.make_async_copy(src, dst, load_sem.at[len(loads)])
        copy.start()
        loads.append(copy)
        return copy

    my_slot = core * 8 + z * 2 + xh
    own_prompt = [
        load(pk_hbm, kv.at[my_slot, :, 0:HEAD]),
        load(pv_hbm, kv.at[my_slot, :, HEAD : 2 * HEAD]),
    ]
    own_keys = []
    for i in range(8):
        rows = pl.ds(i * ROWS, ROWS)
        own_keys.append(load(rk_hbm.at[0, rows], kv.at[16 + i, :, 0:HEAD]))
        own_keys.append(load(rv_hbm.at[0, rows], kv.at[16 + i, :, HEAD : 2 * HEAD]))
    own_q = []
    for g in range(2):
        for h in range(HEADS):
            own_q.append(
                load(q_hbm.at[0, pl.ds(g * GROUP, GROUP), pl.ds(h * HEAD, HEAD)], q.at[g, h])
            )

    position = t * ROWS + lax.broadcasted_iota(jnp.int32, (ROWS, WIDTH), 0)
    live = position < len_ref[0]
    blocks[t] = jnp.where(live, up_ref[0], jnp.zeros((), BF))

    pl.semaphore_wait(barrier, len(peers))

    def g_copy(k, slot, rows, dev):
        ref = blocks.at[slot, pl.ds(rows[0], rows[1])]
        return pltpu.make_async_remote_copy(
            src_ref=ref, dst_ref=ref, send_sem=gs_sem.at[k], recv_sem=gr_sem.at[k],
            device_id=dev, device_id_type=MESH,
        )

    def g_wait(k, slot, rows):
        ref = blocks.at[slot, pl.ds(rows[0], rows[1])]
        pltpu.make_async_remote_copy(
            src_ref=ref, dst_ref=ref, send_sem=gs_sem.at[k], recv_sem=gr_sem.at[k],
            device_id=dev_x, device_id_type=MESH,
        ).wait_recv()

    h0, h1, whole = (0, 32), (32, 32), (0, 64)
    q2, q3 = (32, 16), (48, 16)
    sent = []

    def send(k, slot, rows, dev):
        copy = g_copy(k, slot, rows, dev)
        copy.start()
        sent.append(copy)

    send(0, t, whole, dev_x)
    send(1, t, whole, dev_u)
    send(2, t, whole, dev_d)

    def p_copy(k, src, dst, dev):
        return pltpu.make_async_remote_copy(
            src_ref=src, dst_ref=dst, send_sem=ps_sem.at[k], recv_sem=pr_sem.at[k],
            device_id=dev, device_id_type=MESH,
        )

    for copy in own_prompt:
        copy.wait()
    to_h = p_copy(0, kv.at[my_slot], kv.at[my_slot], dev_h)
    to_h.start()
    wo_load = load(wo_hbm, wo)
    wc_loads = [
        load(wq_hbm, wc.at[:, 0:640]),
        load(wk_hbm, wc.at[:, 640:768]),
        load(wv_hbm, wc.at[:, 768:896]),
    ]
    dkv[...] = jnp.zeros_like(dkv)
    other_slot = core * 8 + z * 2 + 1 - xh
    p_copy(0, kv.at[other_slot], kv.at[other_slot], dev_h).wait_recv()
    to_z = []
    for k in range(3):
        pair = kv.at[pl.ds(core * 8 + z * 2, 2)]
        copy = p_copy(1 + k, pair, pair, dev_z[k])
        copy.start()
        to_z.append(copy)
    for copy in own_keys + own_q:
        copy.wait()
    for k in range(3):
        pair = kv.at[pl.ds(core * 8 + ((z + 3 - k) % 4) * 2, 2)]
        p_copy(1 + k, pair, pair, dev_z[k]).wait_recv()
    lane_half = kv.at[pl.ds(core * 8, 8)]
    to_s = p_copy(4, lane_half, lane_half, dev_s)
    to_s.start()
    other_half = kv.at[pl.ds((1 - core) * 8, 8)]
    p_copy(4, other_half, other_half, dev_s).wait_recv()

    def keys_of(c):
        return kv[pl.ds(c * 4, 4), :, 0:HEAD].reshape(CHUNK, HEAD)

    def values_of(c):
        return kv[pl.ds(c * 4, 4), :, HEAD : 2 * HEAD].reshape(CHUNK, HEAD)

    def flip(c, _):
        kt[c] = keys_of(c).astype(F32).T.astype(BF)
        vt[c] = values_of(c).astype(F32).T.astype(BF)
        return 0

    lax.fori_loop(0, 6, flip, 0)

    scaling = 1.0 / math.sqrt(HEAD)
    to_log2 = scaling * math.log2(math.e)

    def softmax(g):
        count = 5 + g

        def first(c, tops):
            keys = keys_of(c)
            gap = lax.broadcasted_iota(jnp.int32, (CHUNK, GROUP), 0) - lax.broadcasted_iota(
                jnp.int32, (CHUNK, GROUP), 1
            )
            seen = gap <= (g + 4 - c) * CHUNK
            new = []
            for h in range(HEADS):
                s = dot_nt(keys, q[g, h]) * to_log2
                s = jnp.where(seen, s, -1e30)
                scores[c, :, h * GROUP : (h + 1) * GROUP] = s
                new.append(jnp.maximum(tops[h], jnp.max(s, axis=0, keepdims=True)))
            return tuple(new)

        tops = lax.fori_loop(
            0, count, first, tuple(jnp.full((1, GROUP), -1e30, F32) for _ in range(HEADS))
        )

        def second(c, sums):
            new = []
            for h in range(HEADS):
                lanes = slice(h * GROUP, (h + 1) * GROUP)
                e = jnp.exp2(scores[c, :, lanes] - tops[h])
                scores[c, :, lanes] = e
                new.append(sums[h] + jnp.sum(e, axis=0, keepdims=True))
            return tuple(new)

        sums = lax.fori_loop(
            0, count, second, tuple(jnp.zeros((1, GROUP), F32) for _ in range(HEADS))
        )
        inverse = [1.0 / s for s in sums]
        out_t[g] = jnp.zeros((HEAD, LANES), F32)

        def third(c, _):
            for h in range(HEADS):
                lanes = slice(h * GROUP, (h + 1) * GROUP)
                p = (scores[c, :, lanes] * inverse[h]).astype(BF)
                prob[g, c, :, lanes] = p
                out_t[g, :, lanes] += dot(vt[c], p)
            return 0

        lax.fori_loop(0, count, third, 0)

    def attend(g):
        go_acc[...] = jnp.zeros_like(go_acc)

        def project(k, _):
            cols = pl.ds(pl.multiple_of(k * QUARTER, QUARTER), QUARTER)
            rows = blocks[pl.ds(g * 4, 4), :, cols].reshape(GROUP, QUARTER)
            go_acc[...] += dot_nt(rows, wo[:, cols])
            return 0

        lax.fori_loop(0, 4, project, 0)
        for h in range(HEADS):
            lanes = slice(h * GROUP, (h + 1) * GROUP)
            part = go_acc[:, h * HEAD : (h + 1) * HEAD].astype(BF)
            go[g, h] = part
            delta[0:1, lanes] = jnp.sum(
                part.astype(F32).T * out_t[g, :, lanes], axis=0, keepdims=True
            )
        dq_t[...] = jnp.zeros_like(dq_t)

        def step(c, _):
            values = values_of(c)
            for h in range(HEADS):
                lanes = slice(h * GROUP, (h + 1) * GROUP)
                dp = dot_nt(values, go[g, h])
                p = prob[g, c, :, lanes].astype(F32)
                ds[:, lanes] = (p * (dp - delta[0:1, lanes])).astype(BF)
            dk = dot(ds[...], q[g].reshape(LANES, HEAD))
            dv = dot(prob[g, c], go[g].reshape(LANES, HEAD))
            dkv[pl.ds(c * 4, 4), :, 0:HEAD] += dk.reshape(4, ROWS, HEAD)
            dkv[pl.ds(c * 4, 4), :, HEAD : 2 * HEAD] += dv.reshape(4, ROWS, HEAD)
            dq_t[...] += dot(kt[c], ds[...])
            return 0

        lax.fori_loop(0, 5 + g, step, 0)
        for h in range(HEADS):
            dq = (dq_t[:, h * GROUP : (h + 1) * GROUP] * scaling).T.astype(BF)
            grads[pl.ds(pl.multiple_of(g * GROUP, GROUP), GROUP), h * HEAD : (h + 1) * HEAD] = dq

    softmax(xl)

    g_wait(0, i_x, whole)
    g_wait(1, i_d, whole)
    g_wait(2, i_u, whole)
    send(3, i_d, h0, dev_u)
    send(4, i_u, h1, dev_d)
    send(5, i_u, h0, dev_x)
    send(6, i_d, h0, dev_x)
    send(7, i_x, h1, dev_u)
    send(8, i_x, h1, dev_d)

    softmax(ox)
    wo_load.wait()

    g_wait(3, i_f, h0)
    g_wait(4, i_f, h1)
    send(9, i_f, h0, dev_x)

    attend(xl)

    g_wait(5, i_xu, h0)
    g_wait(6, i_xd, h0)
    g_wait(7, i_xd, h1)
    g_wait(8, i_xu, h1)
    send(10, i_xd, q3, dev_u)
    send(11, i_xu, q2, dev_d)
    g_wait(9, i_xf, h0)
    g_wait(10, i_xf, q3)
    g_wait(11, i_xf, q2)
    for copy in sent:
        copy.wait_send()

    attend(ox)
    to_h.wait_send()
    for copy in to_z:
        copy.wait_send()
    to_s.wait_send()
    grads[:, 640:768] = (
        (dkv[16:24, :, 0:HEAD] * scaling).astype(BF).reshape(8 * ROWS, HEAD)
    )
    grads[:, 768:896] = dkv[16:24, :, HEAD : 2 * HEAD].astype(BF).reshape(8 * ROWS, HEAD)

    dkv_scale = jnp.where(
        lax.broadcasted_iota(jnp.int32, (1, 1, 2 * HEAD), 2) < HEAD, scaling, 1.0
    ).astype(F32)
    p_send[...] = (dkv[pl.ds((1 - core) * 8, 8)] * dkv_scale).astype(BF)
    ps = p_copy(5, p_send, p_land, dev_s)
    ps.start()

    for copy in wc_loads:
        copy.wait()
    r_sent = []

    def r_copy(k, src, dst, dev):
        return pltpu.make_async_remote_copy(
            src_ref=src, dst_ref=dst, send_sem=rs_sem.at[k], recv_sem=rr_sem.at[k],
            device_id=dev, device_id_type=MESH,
        )

    low, high = pl.ds(0, HALF), pl.ds(HALF, HALF)
    c2, c3 = pl.ds(2 * QUARTER, QUARTER), pl.ds(3 * QUARTER, QUARTER)
    part = pl.ds(0, QUARTER)

    def r_send(k, slot, cols, dev, narrow=False):
        dst = landed.at[k, :, part] if narrow else landed.at[k]
        copy = r_copy(k, blocks.at[slot, :, cols], dst, dev)
        copy.start()
        r_sent.append(copy)

    def r_wait(k, narrow=False):
        dst = landed.at[k, :, part] if narrow else landed.at[k]
        r_copy(k, dst, dst, dev_x).wait_recv()

    def r_add(k, slot, cols, narrow=False):
        r_wait(k, narrow)
        got = landed[k, :, part] if narrow else landed[k]
        mine = blocks[slot, :, cols]
        blocks[slot, :, cols] = (mine.astype(F32) + got.astype(F32)).astype(BF)

    def term(g, n):
        rows = pl.ds(pl.multiple_of(g * GROUP, GROUP), GROUP)
        for k in range(5):
            start = n * QUARTER + k * 256
            value = dot_nt(grads[rows, :], wc[start : start + 256, :]).astype(BF)
            blocks[pl.ds(g * 4, 4), :, start : start + 256] = value.reshape(4, ROWS, 256)

    term(ox, 0)
    term(ox, 1)
    r_send(0, i_xf, low, dev_x)
    r_send(3, i_xu, low, dev_x)
    r_send(4, i_xd, low, dev_x)
    term(ox, 2)
    r_send(1, i_xf, c2, dev_u, True)
    term(ox, 3)
    r_send(2, i_xf, c3, dev_d, True)
    term(xl, 2)
    term(xl, 3)
    r_send(5, i_f, high, dev_u)
    r_send(9, i_d, high, dev_d)
    r_add(1, i_xu, c2, True)
    r_add(2, i_xd, c3, True)
    r_send(6, i_xu, high, dev_u)
    r_send(7, i_xd, high, dev_d)
    term(xl, 0)
    term(xl, 1)
    r_add(0, i_f, low)
    r_send(8, i_f, low, dev_d)
    r_send(10, i_x, low, dev_x)

    def p_recv(k, dst, dev):
        p_copy(k, dst, dst, dev).wait_recv()

    ps.wait_send()
    p_recv(5, p_land, dev_s)
    mine = dkv.at[pl.ds(core * 8, 8)]
    mine[...] = mine[...] * dkv_scale + p_land[...].astype(F32)
    p_send[...] = mine[...].astype(BF)
    z_copies = []
    for k in range(3):
        peer_z = (z + 1 + k) % 4
        copy = p_copy(6 + k, p_send.at[pl.ds(peer_z * 2, 2)], p_land_z.at[k], dev_z[k])
        copy.start()
        z_copies.append(copy)

    r_add(6, i_x, high)
    r_add(7, i_x, high)
    r_send(11, i_x, high, dev_x)
    r_add(5, i_u, high)
    r_send(12, i_u, high, dev_u)
    r_add(3, i_u, low)
    r_send(13, i_u, low, dev_u)
    r_add(4, i_d, low)
    r_add(8, i_d, low)
    last = r_copy(14, blocks.at[i_d, :, low], landed.at[14], dev_d)
    last.start()
    r_sent.append(last)

    for k in range(3):
        z_copies[k].wait_send()
        p_recv(6 + k, p_land_z.at[k], dev_z[k])
    pair_at = core * 8 + z * 2
    both = dkv[pl.ds(pair_at, 2)]
    for k in range(3):
        both = both + p_land_z[k].astype(F32)
    dkv[pl.ds(pair_at, 2)] = both
    p_send[0] = dkv[pair_at + 1 - xh].astype(BF)
    ph = p_copy(9, p_send.at[0], p_land_h, dev_h)
    ph.start()
    p_recv(9, p_land_h, dev_h)
    total = dkv[pair_at + xh] + p_land_h[...].astype(F32)
    pkg_ref[...] = total[:, 0:HEAD]
    pvg_ref[...] = total[:, HEAD : 2 * HEAD]
    ph.wait_send()

    for k in (9, 10, 11, 12, 13, 14):
        r_wait(k)
    out_ref[0, :, 0:HALF] = (
        (blocks[t, :, low].astype(F32) + landed[10].astype(F32))
        + (landed[13].astype(F32) + landed[14].astype(F32))
    ).astype(BF)
    out_ref[0, :, HALF:WIDTH] = (
        (blocks[t, :, high].astype(F32) + landed[11].astype(F32))
        + (landed[12].astype(F32) + landed[9].astype(F32))
    ).astype(BF)
    for copy in r_sent:
        copy.wait_send()


def body(
    queries,
    response_keys,
    response_values,
    prompt_key_rows,
    prompt_value_rows,
    upstream,
    lengths,
    query_weight,
    key_matrix,
    value_matrix,
    out_weight,
):
    vmem = pl.BlockSpec(memory_space=pltpu.VMEM)
    smem = pl.BlockSpec(memory_space=pltpu.SMEM)
    hbm = pl.BlockSpec(memory_space=pl.ANY)
    dma = pltpu.SemaphoreType.DMA
    return pl.pallas_call(
        kernel,
        out_shape=(
            jax.ShapeDtypeStruct((1, ROWS, WIDTH), BF),
            jax.ShapeDtypeStruct((ROWS, HEAD), F32),
            jax.ShapeDtypeStruct((ROWS, HEAD), F32),
        ),
        in_specs=[smem, hbm, hbm, hbm, hbm, hbm, vmem, hbm, hbm, hbm, hbm],
        out_specs=(vmem, vmem, vmem),
        scratch_shapes=[
            pltpu.VMEM((8, ROWS, WIDTH), BF),
            pltpu.VMEM((HEADS * HEAD, WIDTH), BF),
            pltpu.VMEM((WIDTH, 896), BF),
            pltpu.VMEM((2, HEADS, GROUP, HEAD), BF),
            pltpu.VMEM((24, ROWS, 2 * HEAD), BF),
            pltpu.VMEM((6, HEAD, CHUNK), BF),
            pltpu.VMEM((6, HEAD, CHUNK), BF),
            pltpu.VMEM((6, CHUNK, LANES), F32),
            pltpu.VMEM((2, 6, CHUNK, LANES), BF),
            pltpu.VMEM((2, HEAD, LANES), F32),
            pltpu.VMEM((GROUP, HEADS * HEAD), F32),
            pltpu.VMEM((2, HEADS, GROUP, HEAD), BF),
            pltpu.VMEM((8, LANES), F32),
            pltpu.VMEM((CHUNK, LANES), BF),
            pltpu.VMEM((HEAD, LANES), F32),
            pltpu.VMEM((24, ROWS, 2 * HEAD), F32),
            pltpu.VMEM((8 * ROWS, 896), BF),
            pltpu.VMEM((15, ROWS, HALF), BF),
            pltpu.VMEM((8, ROWS, 2 * HEAD), BF),
            pltpu.VMEM((8, ROWS, 2 * HEAD), BF),
            pltpu.VMEM((3, 2, ROWS, 2 * HEAD), BF),
            pltpu.VMEM((ROWS, 2 * HEAD), BF),
            dma((32,)),
            dma((12,)),
            dma((12,)),
            dma((15,)),
            dma((15,)),
            dma((10,)),
            dma((10,)),
        ],
        compiler_params=pltpu.CompilerParams(
            collective_id=0, has_side_effects=True, vmem_limit_bytes=62 * 1024 * 1024
        ),
        cost_estimate=pl.CostEstimate(
            flops=18_000_000_000, bytes_accessed=20_000_000, transcendentals=4_000_000
        ),
    )(
        lengths,
        queries,
        response_keys,
        response_values,
        prompt_key_rows,
        prompt_value_rows,
        upstream,
        query_weight,
        key_matrix,
        value_matrix,
        out_weight,
    )


def solution(mesh):
    in_specs = (
        P("resp", None, "tp"),
        P("resp", None, "tp"),
        P("resp", None, "tp"),
        P("resp", "tp"),
        P("resp", "tp"),
        P("resp", "tp", None),
        P("resp"),
        P(None, "tp"),
        P(None, "tp"),
        P(None, "tp"),
        P("tp", None),
    )
    out_specs = (P("resp", "tp", None), P("resp", "tp"), P("resp", "tp"))
    return jax.shard_map(body, mesh=mesh, in_specs=in_specs, out_specs=out_specs, check_vma=False)
```

time: 359 us -> 116 us (0.32)
  waiting for transfers between devices: 185 us -> 0 us
  Pallas kernels: 0 us -> 110 us
  matrix products: 73.5 us -> 0 us
  blocking collectives: 51.5 us -> 0 us
  between operations: 14.5 us -> 1.29 us
  other arithmetic: 11.9 us -> 0 us
  loops' own time: 10 us -> 0 us
  local copies, waits for them, and re-layouts: 11.7 us -> 4.71 us
    reduce_scatter x3 -> x0, waiting for transfers between devices: 169 us -> none  [the longest x1 66.6 us: body(): lax.psum_scatter(prompt_value_part.astype(jnp.bfloat16), 'resp', scatter_...]
    pallas_call x0 -> x1, Pallas kernels: none -> 110 us  [body(): pl.pallas_call(kernel, out_shape=(jax.ShapeDtypeStruct((1, ROWS, WIDTH),...]
    dot_general x29 -> x0, matrix products: 73.5 us -> none  [the longest x5 10.3 us: head_backward(): lax.dot_general(probability_b, grad_head, (((0,), (0,)), ((), ())), prefe...]
    all_gather x2 -> x0, blocking collectives: 51.5 us -> none  [the longest x1 29.2 us: body(): lax.all_gather(prompt_key_rows, 'resp', axis=0, tiled=True)]
    all_gather x1 -> x0, waiting for transfers between devices: 15.1 us -> none  [body(): piece_rows = lax.all_gather(upstream, 'tp', axis=1, tiled=True)]
    another operation x1 -> x0, loops' own time: 10 us -> none  [body(): lax.scan(head_step, (zero_sums, zero_sums), jnp.arange(heads_local, dtype...]
    convert_element_type x7 -> x0, other arithmetic: 7.23 us -> none  [the longest x5 4.56 us: head_backward(): (probability * (grad_prob - row_delta) * scaling).astype(jnp.bfloat16)]
    dynamic_update_slice x10 -> x0, local copies, waits for them, and re-layouts: 3.92 us -> none  [body(): lax.scan(head_step, (zero_sums, zero_sums), jnp.arange(heads_local, dtype...]
  transfers between devices with their start and end apart: 4 -> 0, of which waited for: 4 -> 0; matrix products, arithmetic and copies ran while one was open for 9% -> 0% of each run, Pallas kernels for 0% -> 0%
where the time goes in v1:
time: 116 us
  Pallas kernels  110 us (95%)
  local copies, waits for them, and re-layouts  4.71 us (4%)
  between operations  1.29 us (1%)
    pallas_call x1, Pallas kernels, body(): pl.pallas_call(kernel, out_shape=(jax.ShapeDtypeStruct((1, ROWS, WIDTH),...  110 us
    unnamed x3, local copies, waits for them, and re-layouts  4.71 us

profile of v1, /device:TPU:1, one launch (start us, length us, event | category | flops | bytes accessed | tf_op | source)
XLA Modules:
  0.0 115.6 jit_solution(2074185087512542626)
XLA Ops:
  1.3 109.6 %shard_map.130 = (bf16[1,64,5120]{2,1,0:T(8,128)(2,1)}, f32[64,128]{1,0:T(8,128)}, f32[64,128]{1,0:T(8,128)}) custom-call(s32[1]{0:T(128)S(6)} %copy.17.len_ref, bf16[1,512,640]{2,1,0:T(8,128)(2,1)} %q_hbm.1, bf16[1,512,128]{2,1,0:T(8,128)(2,1)} %rk_hbm.1, bf16[1,512,128]{2,1,0:T(8,128)(2,1)} %rv_hbm.1, bf16[64,128]{1,0:T(8,128)(2,1)} %pk_hbm.1, ...), custom_call_target="tpu_custom_call" | custom-call | flops 17999998976 | bytes 20000000 | tf_op jit(solution)/shard_map/pallas_call | solution.py:477
  110.9 2.0 %copy.18 = bf16[1,64,5120]{2,1,0:T(8,128)(2,1)} copy(bf16[1,64,5120]{2,1,0:T(8,128)(2,1)} %get-tuple-element.6) | data formatting | bytes 1310720
  112.8 1.4 %copy.19 = f32[64,128]{1,0:T(8,128)} copy(f32[64,128]{1,0:T(8,128)} %get-tuple-element.7) | data formatting | bytes 65536
  114.2 1.4 %copy.20 = f32[64,128]{1,0:T(8,128)} copy(f32[64,128]{1,0:T(8,128)} %get-tuple-element.8) | data formatting | bytes 65536

commit v2 on v1

v2 whole, which is shorter than its diff:
```python
import functools
import math

import jax
import jax.numpy as jnp
from jax import lax
from jax.experimental import pallas as pl
from jax.experimental.pallas import tpu as pltpu
from jax.sharding import PartitionSpec as P

MESH = pl.DeviceIdType.MESH
BF = jnp.bfloat16
F32 = jnp.float32
WIDTH = 5120
HEADS = 5
HEAD = 128
ROWS = 64
SUB = 128
CHUNK = 256
LANES = HEADS * SUB
QUARTER = WIDTH // 4
PIECE = 16

ORDER = ("o", "U", "D", "X", "F", "XU", "XD", "XF")
POS = {name: i for i, name in enumerate(ORDER)}
RENAME = {
    "X": {"o": "X", "D": "XD", "U": "XU", "F": "XF", "X": "o", "XU": "U", "XD": "D", "XF": "F"},
    "U": {"o": "D", "D": "F", "X": "XD", "XD": "XF", "F": "U", "XF": "XU", "U": "o", "XU": "X"},
    "D": {"o": "U", "U": "F", "X": "XU", "XU": "XF", "F": "D", "XF": "XD", "D": "o", "XD": "X"},
}
W = WIDTH
GATHER = {
    "X": (("o", 3, 0, W), ("o", 2, 0, W), ("o", 1, 0, W), ("o", 0, 0, W), ("D", 0, 0, W), ("D", 1, 0, W),
          ("U", 0, 0, W), ("U", 1, 0, W), ("F", 0, 0, W), ("F", 1, 0, 1792)),
    "U": (("o", 0, 0, W), ("o", 1, 0, W), ("o", 2, 0, W), ("o", 3, 0, W), ("X", 3, 0, W), ("D", 0, 0, W),
          ("D", 1, 0, W), ("X", 2, 0, W), ("XD", 3, 0, W), ("XD", 1, 1792, 1664)),
    "D": (("o", 2, 0, W), ("o", 3, 0, W), ("o", 0, 0, W), ("o", 1, 0, W), ("X", 2, 0, W), ("U", 2, 0, W),
          ("U", 3, 0, W), ("X", 3, 0, W), ("XU", 2, 0, W), ("XU", 1, 3456, 1664)),
}
Q = QUARTER
REDUCE = {
    "X": (("XF", 1, 0, 512), ("XF", 0, 0, Q), ("XU", 1, 0, Q), ("XU", 0, 0, Q), ("XD", 1, 0, Q), ("XD", 0, 0, Q),
          ("X", 0, 0, Q), ("X", 1, 0, Q), ("X", 2, 0, Q), ("X", 3, 0, Q)),
    "U": (("XF", 1, 896, 384), ("XF", 2, 0, Q), ("XU", 3, 0, Q), ("F", 3, 0, Q), ("F", 2, 0, Q), ("XU", 2, 0, Q),
          ("U", 1, 0, Q), ("U", 0, 0, Q), ("U", 3, 0, Q), ("U", 2, 0, Q)),
    "D": (("XF", 1, 512, 384), ("XF", 3, 0, Q), ("XD", 2, 0, Q), ("D", 3, 0, Q), ("D", 2, 0, Q), ("F", 1, 0, Q),
          ("F", 0, 0, Q), ("XD", 3, 0, Q), ("D", 1, 0, Q), ("D", 0, 0, Q)),
}
LINKS = ("X", "U", "D")


def number(plan):
    keys = [(link, i) for link in LINKS for i in range(len(plan[link]))]
    return {key: n for n, key in enumerate(keys)}


def arrivals(plan):
    found = {}
    numbers = number(plan)
    for i in range(10):
        for link in LINKS:
            block, quarter, at, size = plan[link][i]
            key = (RENAME[link][block], quarter)
            found.setdefault(key, []).append((numbers[link, i], at, size))
    return found
NT = (((1,), (1,)), ((), ()))


def dot_nt(a, b):
    return lax.dot_general(a, b, NT, preferred_element_type=F32)


def dot(a, b):
    return jnp.dot(a, b, preferred_element_type=F32)


def kernel(
    len_ref,
    q_hbm,
    rk_hbm,
    rv_hbm,
    pk_hbm,
    pv_hbm,
    up_ref,
    wq_hbm,
    wk_hbm,
    wv_hbm,
    wo_hbm,
    out_ref,
    pg_ref,
    blocks,
    wo,
    wc,
    q,
    kv,
    kt,
    vt,
    scores,
    prob,
    out_t,
    go_acc,
    go,
    delta,
    ds,
    dq_t,
    dkv,
    grads,
    landed,
    p_send,
    p_land,
    p_land_z,
    p_land_h,
    load_sem,
    gs_sem,
    gr_sem,
    rs_sem,
    rr_sem,
    ps_sem,
    pr_sem,
):
    r = lax.axis_index("resp")
    t = lax.axis_index("tp")
    z, xh, core = r // 4, (r // 2) % 2, r % 2
    xl, y = t // 4, t % 4
    up1, down1, far1 = (y + 1) % 4, (y + 3) % 4, (y + 2) % 4
    own, other = xl * 4, (1 - xl) * 4
    ids = [t, own + up1, own + down1, other + y, own + far1, other + up1, other + down1, other + far1]
    device = {"X": (r, ids[3]), "U": (r, ids[1]), "D": (r, ids[2])}
    dev_s = (z * 4 + xh * 2 + 1 - core, t)
    dev_h = (z * 4 + (1 - xh) * 2 + core, t)
    dev_z = [(((z + k) % 4) * 4 + xh * 2 + core, t) for k in (1, 2, 3)]

    barrier = pltpu.get_barrier_semaphore()
    peers = list(device.values()) + [dev_s, dev_h] + dev_z
    for peer in peers:
        pl.semaphore_signal(barrier, inc=1, device_id=peer, device_id_type=MESH)

    loads = []

    def load(src, dst):
        copy = pltpu.make_async_copy(src, dst, load_sem.at[len(loads)])
        copy.start()
        loads.append(copy)
        return copy

    my_slot = core * 8 + z * 2 + xh
    own_prompt = [
        load(pk_hbm, kv.at[my_slot, :, 0:HEAD]),
        load(pv_hbm, kv.at[my_slot, :, HEAD : 2 * HEAD]),
    ]
    own_q = [
        load(
            q_hbm.at[0, pl.ds(pl.multiple_of(ids[p] * ROWS, ROWS), ROWS)],
            grads.at[pl.ds(p * ROWS, ROWS), 0:640],
        )
        for p in range(8)
    ]
    own_keys = []
    for i in range(8):
        rows = pl.ds(i * ROWS, ROWS)
        own_keys.append(load(rk_hbm.at[0, rows], kv.at[16 + i, :, 0:HEAD]))
        own_keys.append(load(rv_hbm.at[0, rows], kv.at[16 + i, :, HEAD : 2 * HEAD]))

    position = t * ROWS + lax.broadcasted_iota(jnp.int32, (ROWS, WIDTH), 0)
    live = position < len_ref[0]
    blocks[0] = jnp.where(live, up_ref[0], jnp.zeros((), BF))

    pl.semaphore_wait(barrier, len(peers))

    def p_copy(k, src, dst, dev):
        return pltpu.make_async_remote_copy(
            src_ref=src, dst_ref=dst, send_sem=ps_sem.at[k], recv_sem=pr_sem.at[k],
            device_id=dev, device_id_type=MESH,
        )

    def p_recv(k, dst, dev):
        p_copy(k, dst, dst, dev).wait_recv()

    for copy in own_prompt:
        copy.wait()
    to_h = p_copy(0, kv.at[my_slot], kv.at[my_slot], dev_h)
    to_h.start()

    g_number, g_arrive = number(GATHER), arrivals(GATHER)
    g_sent, g_seen, g_next = [], set(), {link: 0 for link in LINKS}

    def g_copy(k, src_name, dst_name, quarter, at, size, dev):
        rows, cols = pl.ds(quarter * PIECE, PIECE), pl.ds(at, size)
        return pltpu.make_async_remote_copy(
            src_ref=blocks.at[POS[src_name], rows, cols],
            dst_ref=blocks.at[POS[dst_name], rows, cols],
            send_sem=gs_sem.at[k], recv_sem=gr_sem.at[k], device_id=dev, device_id_type=MESH,
        )

    def g_have(name, quarters=(0, 1, 2, 3)):
        for quarter in quarters:
            if name == "o" or (name, quarter) in g_seen:
                continue
            g_seen.add((name, quarter))
            for k, at, size in g_arrive[name, quarter]:
                g_copy(k, name, name, quarter, at, size, device["X"]).wait_recv()

    def g_send(link, count):
        for _ in range(count):
            i = g_next[link]
            g_next[link] = i + 1
            name, quarter, at, size = GATHER[link][i]
            g_have(name, (quarter,))
            copy = g_copy(
                g_number[link, i], name, RENAME[link][name], quarter, at, size, device[link]
            )
            copy.start()
            g_sent.append(copy)

    for _ in range(4):
        for link in LINKS:
            g_send(link, 1)

    wo_load = load(wo_hbm, wo)
    wc_loads = [
        load(wq_hbm, wc.at[:, 0:640]),
        load(wk_hbm, wc.at[:, 640:768]),
        load(wv_hbm, wc.at[:, 768:896]),
    ]
    p_recv(0, kv.at[core * 8 + z * 2 + 1 - xh], dev_h)
    to_z = []
    for k in range(3):
        pair = kv.at[pl.ds(core * 8 + z * 2, 2)]
        copy = p_copy(1 + k, pair, pair, dev_z[k])
        copy.start()
        to_z.append(copy)
    dkv[...] = jnp.zeros_like(dkv)
    for copy in own_q:
        copy.wait()
    for s in range(4):
        for h in range(HEADS):
            q[s, h] = grads[s * SUB : (s + 1) * SUB, h * HEAD : (h + 1) * HEAD]
    for copy in own_keys:
        copy.wait()

    def keys_of(c):
        return kv[pl.ds(c * 4, 4), :, 0:HEAD].reshape(CHUNK, HEAD)

    def values_of(c):
        return kv[pl.ds(c * 4, 4), :, HEAD : 2 * HEAD].reshape(CHUNK, HEAD)

    def flip(c, _):
        kt[c] = keys_of(c).astype(F32).T.astype(BF)
        vt[c] = values_of(c).astype(F32).T.astype(BF)
        return 0

    lax.fori_loop(4, 6, flip, 0)
    for k in range(3):
        p_recv(1 + k, kv.at[pl.ds(core * 8 + ((z + 3 - k) % 4) * 2, 2)], dev_z[k])
    lane_half = kv.at[pl.ds(core * 8, 8)]
    to_s = p_copy(4, lane_half, lane_half, dev_s)
    to_s.start()
    p_recv(4, kv.at[pl.ds((1 - core) * 8, 8)], dev_s)
    lax.fori_loop(0, 4, flip, 0)

    scaling = 1.0 / math.sqrt(HEAD)
    to_log2 = scaling * math.log2(math.e)

    def softmax(s):
        lane = lax.broadcasted_iota(jnp.int32, (1, SUB), 1)
        row = jnp.where(lane < ROWS, ids[2 * s] * ROWS, ids[2 * s + 1] * ROWS - ROWS) + lane
        q_rows = q[s].reshape(LANES, HEAD)

        def first(c, tops):
            key_at = (c - 4) * CHUNK + lax.broadcasted_iota(jnp.int32, (CHUNK, SUB), 0)
            seen = key_at <= row
            all_heads = dot_nt(keys_of(c), q_rows)
            new = []
            for h in range(HEADS):
                lanes = slice(h * SUB, (h + 1) * SUB)
                part = jnp.where(seen, all_heads[:, lanes] * to_log2, -1e30)
                scores[c, :, lanes] = part
                new.append(jnp.maximum(tops[h], jnp.max(part, axis=0, keepdims=True)))
            return tuple(new)

        tops = lax.fori_loop(
            0, 6, first, tuple(jnp.full((1, SUB), -1e30, F32) for _ in range(HEADS))
        )

        def second(c, sums):
            new = []
            for h in range(HEADS):
                lanes = slice(h * SUB, (h + 1) * SUB)
                e = jnp.exp2(scores[c, :, lanes] - tops[h])
                scores[c, :, lanes] = e
                new.append(sums[h] + jnp.sum(e, axis=0, keepdims=True))
            return tuple(new)

        sums = lax.fori_loop(
            0, 6, second, tuple(jnp.zeros((1, SUB), F32) for _ in range(HEADS))
        )
        inverse = [1.0 / total for total in sums]
        out_t[s] = jnp.zeros((HEAD, LANES), F32)

        def third(c, _):
            for h in range(HEADS):
                lanes = slice(h * SUB, (h + 1) * SUB)
                prob[s, c, :, lanes] = (scores[c, :, lanes] * inverse[h]).astype(BF)
            out_t[s] += dot(vt[c], prob[s, c])
            return 0

        lax.fori_loop(0, 6, third, 0)

    def attend(subs):
        first, count = subs[0], len(subs)
        rows = count * SUB
        go_acc[0:rows] = jnp.zeros((rows, HEADS * HEAD), F32)

        def project(k, _):
            cols = pl.ds(pl.multiple_of(k * QUARTER, QUARTER), QUARTER)
            part = blocks[2 * first : 2 * (first + count), :, cols].reshape(rows, QUARTER)
            go_acc[0:rows] += dot_nt(part, wo[:, cols])
            return 0

        lax.fori_loop(0, 4, project, 0)
        for j, s in enumerate(subs):
            for h in range(HEADS):
                lanes = slice(h * SUB, (h + 1) * SUB)
                part = go_acc[j * SUB : (j + 1) * SUB, h * HEAD : (h + 1) * HEAD].astype(BF)
                go[s, h] = part
                delta[s, 0:1, lanes] = jnp.sum(
                    part.astype(F32).T * out_t[s, :, lanes], axis=0, keepdims=True
                )
        wide = count * LANES
        dq_t[:, 0:wide] = jnp.zeros((HEAD, wide), F32)

        def step(c, _):
            values = values_of(c)
            dv = jnp.zeros((CHUNK, HEAD), F32)
            for j, s in enumerate(subs):
                dp = dot_nt(values, go[s].reshape(LANES, HEAD))
                for h in range(HEADS):
                    lanes = slice(h * SUB, (h + 1) * SUB)
                    p = prob[s, c, :, lanes].astype(F32)
                    ds[:, j * LANES + h * SUB : j * LANES + (h + 1) * SUB] = (
                        p * (dp[:, lanes] - delta[s, 0:1, lanes])
                    ).astype(BF)
                dv = dv + dot(prob[s, c], go[s].reshape(LANES, HEAD))
            dk = dot(ds[:, 0:wide], q[first : first + count].reshape(wide, HEAD))
            dkv[pl.ds(c * 4, 4), :, 0:HEAD] += dk.reshape(4, ROWS, HEAD)
            dkv[pl.ds(c * 4, 4), :, HEAD : 2 * HEAD] += dv.reshape(4, ROWS, HEAD)
            dq_t[:, 0:wide] += dot(kt[c], ds[:, 0:wide])
            return 0

        lax.fori_loop(0, 6, step, 0)
        for j, s in enumerate(subs):
            for h in range(HEADS):
                at = j * LANES + h * SUB
                grads[s * SUB : (s + 1) * SUB, h * HEAD : (h + 1) * HEAD] = (
                    (dq_t[:, at : at + SUB] * scaling).T.astype(BF)
                )

    for link in ("U", "D"):
        g_send(link, 4)
    g_send("X", 2)
    softmax(0)
    softmax(1)
    wo_load.wait()
    g_send("X", 2)
    for name in ("U", "D", "X"):
        g_have(name)
    attend((0, 1))
    softmax(2)
    for link in ("X", "U", "D"):
        g_send(link, 2)
    softmax(3)
    g_have("F")
    g_have("XU")
    attend((2,))
    g_have("XD")
    g_have("XF")
    for copy in g_sent:
        copy.wait_send()
    attend((3,))
    to_h.wait_send()
    for copy in to_z:
        copy.wait_send()
    to_s.wait_send()

    dkv_scale = jnp.where(
        lax.broadcasted_iota(jnp.int32, (1, 1, 2 * HEAD), 2) < HEAD, scaling, 1.0
    ).astype(F32)
    for p in range(8):
        grads[p * ROWS : (p + 1) * ROWS, 640:896] = (dkv[16 + ids[p]] * dkv_scale[0]).astype(BF)
    for copy in wc_loads:
        copy.wait()

    r_number, r_arrive = number(REDUCE), arrivals(REDUCE)
    r_sent, r_seen, r_next = [], set(), {link: 0 for link in LINKS}

    def r_copy(k, src, size, dev):
        return pltpu.make_async_remote_copy(
            src_ref=src, dst_ref=landed.at[k, :, pl.ds(0, size)],
            send_sem=rs_sem.at[k], recv_sem=rr_sem.at[k], device_id=dev, device_id_type=MESH,
        )

    def r_wait(k, size):
        r_copy(k, landed.at[k, :, pl.ds(0, size)], size, device["X"]).wait_recv()

    def r_add(name, quarter):
        if (name, quarter) in r_seen:
            return
        r_seen.add((name, quarter))
        for k, at, size in r_arrive.get((name, quarter), ()):
            r_wait(k, size)
            cols = pl.ds(quarter * QUARTER + at, size)
            mine = blocks[POS[name], :, cols].astype(F32)
            blocks[POS[name], :, cols] = (mine + landed[k, :, 0:size].astype(F32)).astype(BF)

    def r_send(link, count):
        for _ in range(count):
            i = r_next[link]
            r_next[link] = i + 1
            name, quarter, at, size = REDUCE[link][i]
            r_add(name, quarter)
            k = r_number[link, i]
            src = blocks.at[POS[name], :, pl.ds(quarter * QUARTER + at, size)]
            copy = r_copy(k, src, size, device[link])
            copy.start()
            r_sent.append(copy)

    def term(half, quarter):
        rows = slice(half * 256, half * 256 + 256)
        for k in range(5):
            start = quarter * QUARTER + k * 256
            value = dot_nt(grads[rows, :], wc[start : start + 256, :]).astype(BF)
            blocks[half * 4 : half * 4 + 4, :, start : start + 256] = value.reshape(4, ROWS, 256)

    term(1, 1)
    for link in LINKS:
        r_send(link, 1)
    term(1, 2)
    r_send("U", 1)
    term(1, 3)
    r_send("D", 1)
    r_send("U", 2)
    term(1, 0)
    r_send("X", 5)
    r_send("U", 1)
    r_send("D", 1)
    p_send[...] = (dkv[pl.ds((1 - core) * 8, 8)] * dkv_scale).astype(BF)
    ps = p_copy(5, p_send, p_land, dev_s)
    ps.start()
    term(0, 3)
    r_send("D", 1)
    term(0, 2)
    r_send("D", 1)
    term(0, 0)
    term(0, 1)
    r_send("D", 3)
    r_send("U", 1)
    r_send("X", 2)

    ps.wait_send()
    p_recv(5, p_land, dev_s)
    mine = pl.ds(core * 8, 8)
    dkv[mine] = dkv[mine] * dkv_scale + p_land[...].astype(F32)
    p_send[...] = dkv[mine].astype(BF)
    z_copies = []
    for k in range(3):
        peer_z = (z + 1 + k) % 4
        copy = p_copy(6 + k, p_send.at[pl.ds(peer_z * 2, 2)], p_land_z.at[k], dev_z[k])
        copy.start()
        z_copies.append(copy)

    r_send("U", 4)

    for k in range(3):
        z_copies[k].wait_send()
        p_recv(6 + k, p_land_z.at[k], dev_z[k])
    pair_at = core * 8 + z * 2
    both = dkv[pl.ds(pair_at, 2)]
    for k in range(3):
        both = both + p_land_z[k].astype(F32)
    dkv[pl.ds(pair_at, 2)] = both
    p_send[0] = dkv[pair_at + 1 - xh].astype(BF)
    ph = p_copy(9, p_send.at[0], p_land_h, dev_h)
    ph.start()

    r_send("D", 2)
    r_send("X", 1)
    p_recv(9, p_land_h, dev_h)
    pg_ref[...] = dkv[pair_at + xh] + p_land_h[...].astype(F32)
    r_send("X", 1)
    ph.wait_send()

    for quarter in (0, 1, 2, 3):
        cols = slice(quarter * QUARTER, (quarter + 1) * QUARTER)
        total = blocks[0, :, cols].astype(F32)
        for k, at, size in r_arrive["o", quarter]:
            r_wait(k, size)
            total = total + landed[k].astype(F32)
        out_ref[0, :, cols] = total.astype(BF)
    for copy in r_sent:
        copy.wait_send()


def split_kernel(rows_ref, both_ref, out_ref, key_ref, value_ref):
    out_ref[...] = rows_ref[...]
    key_ref[...] = both_ref[:, 0:HEAD]
    value_ref[...] = both_ref[:, HEAD : 2 * HEAD]


def split(input_grad, prompt_grads):
    vmem = pl.BlockSpec(memory_space=pltpu.VMEM)
    return pl.pallas_call(
        split_kernel,
        out_shape=(
            jax.ShapeDtypeStruct((1, ROWS, WIDTH), BF),
            jax.ShapeDtypeStruct((ROWS, HEAD), F32),
            jax.ShapeDtypeStruct((ROWS, HEAD), F32),
        ),
        in_specs=[vmem, vmem],
        out_specs=(vmem, vmem, vmem),
    )(input_grad, prompt_grads)


def body(
    queries,
    response_keys,
    response_values,
    prompt_key_rows,
    prompt_value_rows,
    upstream,
    lengths,
    query_weight,
    key_matrix,
    value_matrix,
    out_weight,
):
    vmem = pl.BlockSpec(memory_space=pltpu.VMEM)
    smem = pl.BlockSpec(memory_space=pltpu.SMEM)
    hbm = pl.BlockSpec(memory_space=pl.ANY)
    dma = pltpu.SemaphoreType.DMA
    input_grad, prompt_grads = pl.pallas_call(
        kernel,
        out_shape=(
            jax.ShapeDtypeStruct((1, ROWS, WIDTH), BF),
            jax.ShapeDtypeStruct((ROWS, 2 * HEAD), F32),
        ),
        in_specs=[smem, hbm, hbm, hbm, hbm, hbm, vmem, hbm, hbm, hbm, hbm],
        out_specs=(vmem, vmem),
        scratch_shapes=[
            pltpu.VMEM((8, ROWS, WIDTH), BF),
            pltpu.VMEM((HEADS * HEAD, WIDTH), BF),
            pltpu.VMEM((WIDTH, 896), BF),
            pltpu.VMEM((4, HEADS, SUB, HEAD), BF),
            pltpu.VMEM((24, ROWS, 2 * HEAD), BF),
            pltpu.VMEM((6, HEAD, CHUNK), BF),
            pltpu.VMEM((6, HEAD, CHUNK), BF),
            pltpu.VMEM((6, CHUNK, LANES), F32),
            pltpu.VMEM((4, 6, CHUNK, LANES), BF),
            pltpu.VMEM((4, HEAD, LANES), F32),
            pltpu.VMEM((2 * SUB, HEADS * HEAD), F32),
            pltpu.VMEM((4, HEADS, SUB, HEAD), BF),
            pltpu.VMEM((4, 8, LANES), F32),
            pltpu.VMEM((CHUNK, 2 * LANES), BF),
            pltpu.VMEM((HEAD, 2 * LANES), F32),
            pltpu.VMEM((24, ROWS, 2 * HEAD), F32),
            pltpu.VMEM((8 * ROWS, 896), BF),
            pltpu.VMEM((30, ROWS, QUARTER), BF),
            pltpu.VMEM((8, ROWS, 2 * HEAD), BF),
            pltpu.VMEM((8, ROWS, 2 * HEAD), BF),
            pltpu.VMEM((3, 2, ROWS, 2 * HEAD), BF),
            pltpu.VMEM((ROWS, 2 * HEAD), BF),
            dma((32,)),
            dma((30,)),
            dma((30,)),
            dma((30,)),
            dma((30,)),
            dma((10,)),
            dma((10,)),
        ],
        compiler_params=pltpu.CompilerParams(
            collective_id=0, has_side_effects=True, vmem_limit_bytes=62 * 1024 * 1024
        ),
        cost_estimate=pl.CostEstimate(
            flops=18_000_000_000, bytes_accessed=20_000_000, transcendentals=4_000_000
        ),
    )(
        lengths,
        queries,
        response_keys,
        response_values,
        prompt_key_rows,
        prompt_value_rows,
        upstream,
        query_weight,
        key_matrix,
        value_matrix,
        out_weight,
    )
    return split(input_grad, prompt_grads)


def solution(mesh):
    in_specs = (
        P("resp", None, "tp"),
        P("resp", None, "tp"),
        P("resp", None, "tp"),
        P("resp", "tp"),
        P("resp", "tp"),
        P("resp", "tp", None),
        P("resp"),
        P(None, "tp"),
        P(None, "tp"),
        P(None, "tp"),
        P("tp", None),
    )
    out_specs = (P("resp", "tp", None), P("resp", "tp"), P("resp", "tp"))
    return jax.shard_map(body, mesh=mesh, in_specs=in_specs, out_specs=out_specs, check_vma=False)
```

time: 116 us -> 98.2 us (0.85)
  Pallas kernels: 110 us -> 96.7 us
  local copies, waits for them, and re-layouts: 4.71 us -> 0 us
    pallas_call x1, Pallas kernels: 110 us -> 94.7 us  [body(): pl.pallas_call(kernel, out_shape=(jax.ShapeDtypeStruct((1, ROWS, WIDTH),...]
    unnamed x3 -> x0, local copies, waits for them, and re-layouts: 4.71 us -> none
    pallas_call x0 -> x1, Pallas kernels: none -> 1.97 us  [split(): pl.pallas_call(split_kernel, out_shape=(jax.ShapeDtypeStruct((1, ROWS, WI...]
where the time goes in v2:
time: 98.2 us; the launch traced here: 98 us
  Pallas kernels  96.7 us (98%)
  between operations  1.29 us (1%)
    pallas_call x1, Pallas kernels, body(): pl.pallas_call(kernel, out_shape=(jax.ShapeDtypeStruct((1, ROWS, WIDTH),...  94.7 us
    pallas_call x1, Pallas kernels, split(): pl.pallas_call(split_kernel, out_shape=(jax.ShapeDtypeStruct((1, ROWS, WI...  1.97 us

profile of v2, /device:TPU:1, one launch (start us, length us, event | category | flops | bytes accessed | tf_op | source)
XLA Modules:
  0.0 98.0 jit_solution(16028378678652297853)
XLA Ops:
  1.3 94.7 %shard_map.130 = (bf16[1,64,5120]{2,1,0:T(8,128)(2,1)}, f32[64,256]{1,0:T(8,128)}) custom-call(s32[1]{0:T(128)S(6)} %copy.14.len_ref, bf16[1,512,640]{2,1,0:T(8,128)(2,1)} %q_hbm.1, bf16[1,512,128]{2,1,0:T(8,128)(2,1)} %rk_hbm.1, bf16[1,512,128]{2,1,0:T(8,128)(2,1)} %rv_hbm.1, bf16[64,128]{1,0:T(8,128)(2,1)} %pk_hbm.1, bf16[64,128]{1,0:T(8,128)(2,1)} %pv_hbm.1, ...), custom_call_target="tpu_custom_call" | custom-call | flops 17999998976 | bytes 20000000 | tf_op jit(solution)/shard_map/pallas_call | solution.py:540
  96.0 2.0 %shard_map.131 = (bf16[1,64,5120]{2,1,0:T(8,128)(2,1)}, f32[64,128]{1,0:T(8,128)}, f32[64,128]{1,0:T(8,128)}) custom-call(bf16[1,64,5120]{2,1,0:T(8,128)(2,1)} %get-tuple-element.5.rows_ref, f32[64,256]{1,0:T(8,128)} %get-tuple-element.6.both_ref), custom_call_target="tpu_custom_call" | custom-call | tf_op jit(solution)/shard_map/pallas_call | solution.py:511

commit v3 on v2

--- a/solution.py
+++ b/solution.py
@@ -19,7 +19,6 @@
 CHUNK = 256
 LANES = HEADS * SUB
 QUARTER = WIDTH // 4
-PIECE = 16
 
 ORDER = ("o", "U", "D", "X", "F", "XU", "XD", "XF")
 POS = {name: i for i, name in enumerate(ORDER)}
@@ -28,22 +27,23 @@
     "U": {"o": "D", "D": "F", "X": "XD", "XD": "XF", "F": "U", "XF": "XU", "U": "o", "XU": "X"},
     "D": {"o": "U", "U": "F", "X": "XU", "XU": "XF", "F": "D", "XF": "XD", "D": "o", "XD": "X"},
 }
-W = WIDTH
+Q = QUARTER
+A = 896
+B = Q - A
 GATHER = {
-    "X": (("o", 3, 0, W), ("o", 2, 0, W), ("o", 1, 0, W), ("o", 0, 0, W), ("D", 0, 0, W), ("D", 1, 0, W),
-          ("U", 0, 0, W), ("U", 1, 0, W), ("F", 0, 0, W), ("F", 1, 0, 1792)),
-    "U": (("o", 0, 0, W), ("o", 1, 0, W), ("o", 2, 0, W), ("o", 3, 0, W), ("X", 3, 0, W), ("D", 0, 0, W),
-          ("D", 1, 0, W), ("X", 2, 0, W), ("XD", 3, 0, W), ("XD", 1, 1792, 1664)),
-    "D": (("o", 2, 0, W), ("o", 3, 0, W), ("o", 0, 0, W), ("o", 1, 0, W), ("X", 2, 0, W), ("U", 2, 0, W),
-          ("U", 3, 0, W), ("X", 3, 0, W), ("XU", 2, 0, W), ("XU", 1, 3456, 1664)),
+    "X": (("o", 3, 0, Q), ("o", 2, 0, Q), ("o", 1, 0, Q), ("o", 0, 0, Q), ("D", 0, 0, A), ("D", 1, 0, Q),
+          ("U", 0, 0, A), ("U", 1, 0, Q), ("F", 0, 0, Q), ("F", 1, 0, Q)),
+    "U": (("o", 0, 0, Q), ("o", 1, 0, Q), ("o", 2, 0, Q), ("o", 3, 0, Q), ("X", 3, 0, Q), ("D", 0, 0, Q),
+          ("D", 1, 0, Q), ("X", 0, A, B), ("X", 2, 0, Q), ("XD", 3, 0, Q)),
+    "D": (("o", 2, 0, Q), ("o", 3, 0, Q), ("o", 0, 0, Q), ("o", 1, 0, Q), ("X", 2, 0, Q), ("U", 2, 0, Q),
+          ("U", 3, 0, Q), ("X", 0, A, B), ("X", 3, 0, Q), ("XU", 2, 0, Q)),
 }
-Q = QUARTER
 REDUCE = {
-    "X": (("XF", 1, 0, 512), ("XF", 0, 0, Q), ("XU", 1, 0, Q), ("XU", 0, 0, Q), ("XD", 1, 0, Q), ("XD", 0, 0, Q),
-          ("X", 0, 0, Q), ("X", 1, 0, Q), ("X", 2, 0, Q), ("X", 3, 0, Q)),
-    "U": (("XF", 1, 896, 384), ("XF", 2, 0, Q), ("XU", 3, 0, Q), ("F", 3, 0, Q), ("F", 2, 0, Q), ("XU", 2, 0, Q),
+    "X": (("XF", 1, 0, Q), ("XU", 1, 0, Q), ("XD", 1, 0, Q), ("XF", 0, 0, Q), ("XU", 0, 0, A), ("XD", 0, 0, A),
+          ("X", 1, 0, Q), ("X", 2, 0, Q), ("X", 0, 0, Q), ("X", 3, 0, Q)),
+    "U": (("XU", 3, 0, Q), ("F", 3, 0, Q), ("XF", 2, 0, Q), ("F", 2, 0, Q), ("XU", 0, A, B), ("XU", 2, 0, Q),
           ("U", 1, 0, Q), ("U", 0, 0, Q), ("U", 3, 0, Q), ("U", 2, 0, Q)),
-    "D": (("XF", 1, 512, 384), ("XF", 3, 0, Q), ("XD", 2, 0, Q), ("D", 3, 0, Q), ("D", 2, 0, Q), ("F", 1, 0, Q),
+    "D": (("XF", 3, 0, Q), ("XD", 2, 0, Q), ("D", 3, 0, Q), ("D", 2, 0, Q), ("XD", 0, A, B), ("F", 1, 0, Q),
           ("F", 0, 0, Q), ("XD", 3, 0, Q), ("D", 1, 0, Q), ("D", 0, 0, Q)),
 }
 LINKS = ("X", "U", "D")
@@ -63,6 +63,8 @@
             key = (RENAME[link][block], quarter)
             found.setdefault(key, []).append((numbers[link, i], at, size))
     return found
+
+
 NT = (((1,), (1,)), ((), ()))
 
 
@@ -99,6 +101,7 @@
     prob,
     out_t,
     go_acc,
+    inv,
     go,
     delta,
     ds,
@@ -185,10 +188,10 @@
     g_sent, g_seen, g_next = [], set(), {link: 0 for link in LINKS}
 
     def g_copy(k, src_name, dst_name, quarter, at, size, dev):
-        rows, cols = pl.ds(quarter * PIECE, PIECE), pl.ds(at, size)
+        cols = pl.ds(quarter * QUARTER + at, size)
         return pltpu.make_async_remote_copy(
-            src_ref=blocks.at[POS[src_name], rows, cols],
-            dst_ref=blocks.at[POS[dst_name], rows, cols],
+            src_ref=blocks.at[POS[src_name], :, cols],
+            dst_ref=blocks.at[POS[dst_name], :, cols],
             send_sem=gs_sem.at[k], recv_sem=gr_sem.at[k], device_id=dev, device_id_type=MESH,
         )
 
@@ -273,81 +276,86 @@
             new = []
             for h in range(HEADS):
                 lanes = slice(h * SUB, (h + 1) * SUB)
-                part = jnp.where(seen, all_heads[:, lanes] * to_log2, -1e30)
+                part = jnp.where(seen, all_heads[:, lanes], -1e30)
                 scores[c, :, lanes] = part
                 new.append(jnp.maximum(tops[h], jnp.max(part, axis=0, keepdims=True)))
             return tuple(new)
 
         tops = lax.fori_loop(
-            0, 6, first, tuple(jnp.full((1, SUB), -1e30, F32) for _ in range(HEADS))
+            0, 6, first, tuple(jnp.full((1, SUB), -1e30, F32) for _ in range(HEADS)), unroll=3
         )
+        out_t[s] = jnp.zeros((HEAD, LANES), F32)
 
         def second(c, sums):
             new = []
             for h in range(HEADS):
                 lanes = slice(h * SUB, (h + 1) * SUB)
-                e = jnp.exp2(scores[c, :, lanes] - tops[h])
-                scores[c, :, lanes] = e
+                e = jnp.exp2((scores[c, :, lanes] - tops[h]) * to_log2)
+                prob[s, c, :, lanes] = e.astype(BF)
                 new.append(sums[h] + jnp.sum(e, axis=0, keepdims=True))
+            out_t[s] += dot(vt[c], prob[s, c])
             return tuple(new)
 
         sums = lax.fori_loop(
-            0, 6, second, tuple(jnp.zeros((1, SUB), F32) for _ in range(HEADS))
+            0, 6, second, tuple(jnp.zeros((1, SUB), F32) for _ in range(HEADS)), unroll=3
         )
-        inverse = [1.0 / total for total in sums]
-        out_t[s] = jnp.zeros((HEAD, LANES), F32)
-
-        def third(c, _):
+        for h in range(HEADS):
+            lanes = slice(h * SUB, (h + 1) * SUB)
+            inverse = 1.0 / sums[h]
+            out_t[s, :, lanes] = out_t[s, :, lanes] * inverse
+            inv[s, h] = jnp.broadcast_to(inverse, (SUB, HEAD)).T
+
+    def project(subs):
+        first, count = subs[0], len(subs)
+        rows = count * SUB
+        for at, size in ((0, 256), (256, 256), (512, 128)):
+            part = blocks[2 * first : 2 * (first + count)].reshape(rows, WIDTH)
+            go_acc[first * SUB : first * SUB + rows, at : at + size] = dot_nt(
+                part, wo[at : at + size, :]
+            )
+
+    def project_part(s, quarter, start):
+        cols = slice(quarter * QUARTER, (quarter + 1) * QUARTER)
+        rows = slice(s * SUB, (s + 1) * SUB)
+        part = dot_nt(blocks[2 * s : 2 * s + 2, :, cols].reshape(SUB, QUARTER), wo[:, cols])
+        if start:
+            go_acc[rows] = part
+        else:
+            go_acc[rows] += part
+
+    def attend(subs):
+        first, count = subs[0], len(subs)
+        for s in subs:
             for h in range(HEADS):
                 lanes = slice(h * SUB, (h + 1) * SUB)
-                prob[s, c, :, lanes] = (scores[c, :, lanes] * inverse[h]).astype(BF)
-            out_t[s] += dot(vt[c], prob[s, c])
-            return 0
-
-        lax.fori_loop(0, 6, third, 0)
-
-    def attend(subs):
-        first, count = subs[0], len(subs)
-        rows = count * SUB
-        go_acc[0:rows] = jnp.zeros((rows, HEADS * HEAD), F32)
-
-        def project(k, _):
-            cols = pl.ds(pl.multiple_of(k * QUARTER, QUARTER), QUARTER)
-            part = blocks[2 * first : 2 * (first + count), :, cols].reshape(rows, QUARTER)
-            go_acc[0:rows] += dot_nt(part, wo[:, cols])
-            return 0
-
-        lax.fori_loop(0, 4, project, 0)
-        for j, s in enumerate(subs):
-            for h in range(HEADS):
-                lanes = slice(h * SUB, (h + 1) * SUB)
-                part = go_acc[j * SUB : (j + 1) * SUB, h * HEAD : (h + 1) * HEAD].astype(BF)
-                go[s, h] = part
+                part = go_acc[s * SUB : (s + 1) * SUB, h * HEAD : (h + 1) * HEAD] * inv[s, h]
+                go[s, h] = part.astype(BF)
                 delta[s, 0:1, lanes] = jnp.sum(
-                    part.astype(F32).T * out_t[s, :, lanes], axis=0, keepdims=True
+                    part.T * out_t[s, :, lanes], axis=0, keepdims=True
                 )
         wide = count * LANES
         dq_t[:, 0:wide] = jnp.zeros((HEAD, wide), F32)
 
         def step(c, _):
             values = values_of(c)
-            dv = jnp.zeros((CHUNK, HEAD), F32)
+            dv = None
             for j, s in enumerate(subs):
                 dp = dot_nt(values, go[s].reshape(LANES, HEAD))
                 for h in range(HEADS):
                     lanes = slice(h * SUB, (h + 1) * SUB)
-                    p = prob[s, c, :, lanes].astype(F32)
+                    e = prob[s, c, :, lanes].astype(F32)
                     ds[:, j * LANES + h * SUB : j * LANES + (h + 1) * SUB] = (
-                        p * (dp[:, lanes] - delta[s, 0:1, lanes])
+                        e * (dp[:, lanes] - delta[s, 0:1, lanes])
                     ).astype(BF)
-                dv = dv + dot(prob[s, c], go[s].reshape(LANES, HEAD))
+                part = dot(prob[s, c], go[s].reshape(LANES, HEAD))
+                dv = part if dv is None else dv + part
             dk = dot(ds[:, 0:wide], q[first : first + count].reshape(wide, HEAD))
             dkv[pl.ds(c * 4, 4), :, 0:HEAD] += dk.reshape(4, ROWS, HEAD)
             dkv[pl.ds(c * 4, 4), :, HEAD : 2 * HEAD] += dv.reshape(4, ROWS, HEAD)
             dq_t[:, 0:wide] += dot(kt[c], ds[:, 0:wide])
             return 0
 
-        lax.fori_loop(0, 6, step, 0)
+        lax.fori_loop(0, 6, step, 0, unroll=3)
         for j, s in enumerate(subs):
             for h in range(HEADS):
                 at = j * LANES + h * SUB
@@ -356,27 +364,34 @@
                 )
 
     for link in ("U", "D"):
-        g_send(link, 4)
+        g_send(link, 3)
     g_send("X", 2)
     softmax(0)
     softmax(1)
     wo_load.wait()
-    g_send("X", 2)
+    for link in LINKS:
+        g_send(link, 2)
     for name in ("U", "D", "X"):
         g_have(name)
+    project((0, 1))
     attend((0, 1))
     softmax(2)
-    for link in ("X", "U", "D"):
-        g_send(link, 2)
+    for link in LINKS:
+        g_send(link, 1)
     softmax(3)
-    g_have("F")
-    g_have("XU")
+    g_send("X", 1)
+    for n, quarter in enumerate((0, 1, 2, 3)):
+        g_have("F", (quarter,))
+        g_have("XU", (quarter,))
+        project_part(2, quarter, n == 0)
     attend((2,))
-    g_have("XD")
-    g_have("XF")
+    for n, quarter in enumerate((0, 2, 3, 1)):
+        g_have("XD", (quarter,))
+        g_have("XF", (quarter,))
+        project_part(3, quarter, n == 0)
+    attend((3,))
     for copy in g_sent:
         copy.wait_send()
-    attend((3,))
     to_h.wait_send()
     for copy in to_z:
         copy.wait_send()
@@ -432,29 +447,27 @@
             blocks[half * 4 : half * 4 + 4, :, start : start + 256] = value.reshape(4, ROWS, 256)
 
     term(1, 1)
-    for link in LINKS:
-        r_send(link, 1)
+    r_send("X", 3)
+    term(1, 3)
+    r_send("U", 2)
+    r_send("D", 1)
     term(1, 2)
+    r_send("U", 2)
+    r_send("D", 1)
+    term(1, 0)
+    r_send("X", 3)
     r_send("U", 1)
-    term(1, 3)
-    r_send("D", 1)
-    r_send("U", 2)
-    term(1, 0)
-    r_send("X", 5)
-    r_send("U", 1)
-    r_send("D", 1)
     p_send[...] = (dkv[pl.ds((1 - core) * 8, 8)] * dkv_scale).astype(BF)
     ps = p_copy(5, p_send, p_land, dev_s)
     ps.start()
     term(0, 3)
     r_send("D", 1)
     term(0, 2)
+    r_send("D", 2)
+    term(0, 1)
+    r_send("X", 1)
     r_send("D", 1)
     term(0, 0)
-    term(0, 1)
-    r_send("D", 3)
-    r_send("U", 1)
-    r_send("X", 2)
 
     ps.wait_send()
     p_recv(5, p_land, dev_s)
@@ -468,7 +481,7 @@
         copy.start()
         z_copies.append(copy)
 
-    r_send("U", 4)
+    r_send("U", 2)
 
     for k in range(3):
         z_copies[k].wait_send()
@@ -483,9 +496,11 @@
     ph.start()
 
     r_send("D", 2)
-    r_send("X", 1)
+    r_send("U", 3)
     p_recv(9, p_land_h, dev_h)
     pg_ref[...] = dkv[pair_at + xh] + p_land_h[...].astype(F32)
+    r_send("X", 2)
+    r_send("D", 2)
     r_send("X", 1)
     ph.wait_send()
 
@@ -556,7 +571,8 @@
             pltpu.VMEM((6, CHUNK, LANES), F32),
             pltpu.VMEM((4, 6, CHUNK, LANES), BF),
             pltpu.VMEM((4, HEAD, LANES), F32),
-            pltpu.VMEM((2 * SUB, HEADS * HEAD), F32),
+            pltpu.VMEM((4 * SUB, HEADS * HEAD), F32),
+            pltpu.VMEM((4, HEADS, SUB, HEAD), F32),
             pltpu.VMEM((4, HEADS, SUB, HEAD), BF),
             pltpu.VMEM((4, 8, LANES), F32),
             pltpu.VMEM((CHUNK, 2 * LANES), BF),

time: 98.2 us -> 87.8 us (0.89); the launches traced: 98 us -> 86.6 us
  Pallas kernels: 96.7 us -> 85.3 us
    pallas_call x1, Pallas kernels: 94.7 us -> 83.3 us  [body(): pl.pallas_call(kernel, out_shape=(jax.ShapeDtypeStruct((1, ROWS, WIDTH),...]
where the time goes in v3:
time: 87.8 us; the launch traced here: 86.6 us
  Pallas kernels  85.3 us (97%)
  between operations  1.29 us (1%)
    pallas_call x1, Pallas kernels, body(): pl.pallas_call(kernel, out_shape=(jax.ShapeDtypeStruct((1, ROWS, WIDTH),...  83.3 us
    pallas_call x1, Pallas kernels, split(): pl.pallas_call(split_kernel, out_shape=(jax.ShapeDtypeStruct((1, ROWS, WI...  1.97 us

profile of v3, /device:TPU:1, one launch (start us, length us, event | category | flops | bytes accessed | tf_op | source)
XLA Modules:
  0.0 86.6 jit_solution(207204153212313353)
XLA Ops:
  1.3 83.3 %shard_map.130 = (bf16[1,64,5120]{2,1,0:T(8,128)(2,1)}, f32[64,256]{1,0:T(8,128)}) custom-call(s32[1]{0:T(128)S(6)} %copy.14.len_ref, bf16[1,512,640]{2,1,0:T(8,128)(2,1)} %q_hbm.1, bf16[1,512,128]{2,1,0:T(8,128)(2,1)} %rk_hbm.1, bf16[1,512,128]{2,1,0:T(8,128)(2,1)} %rv_hbm.1, bf16[64,128]{1,0:T(8,128)(2,1)} %pk_hbm.1, bf16[64,128]{1,0:T(8,128)(2,1)} %pv_hbm.1, ...), custom_call_target="tpu_custom_call" | custom-call | flops 17999998976 | bytes 20000000 | tf_op jit(solution)/shard_map/pallas_call | solution.py:555
  84.6 2.0 %shard_map.131 = (bf16[1,64,5120]{2,1,0:T(8,128)(2,1)}, f32[64,128]{1,0:T(8,128)}, f32[64,128]{1,0:T(8,128)}) custom-call(bf16[1,64,5120]{2,1,0:T(8,128)(2,1)} %get-tuple-element.5.rows_ref, f32[64,256]{1,0:T(8,128)} %get-tuple-element.6.both_ref), custom_call_target="tpu_custom_call" | custom-call | tf_op jit(solution)/shard_map/pallas_call | solution.py:526

commit v4 on v3

--- a/solution.py
+++ b/solution.py
@@ -38,12 +38,14 @@
     "D": (("o", 2, 0, Q), ("o", 3, 0, Q), ("o", 0, 0, Q), ("o", 1, 0, Q), ("X", 2, 0, Q), ("U", 2, 0, Q),
           ("U", 3, 0, Q), ("X", 0, A, B), ("X", 3, 0, Q), ("XU", 2, 0, Q)),
 }
+A2 = 1024
+B2 = Q - A2
 REDUCE = {
-    "X": (("XF", 1, 0, Q), ("XU", 1, 0, Q), ("XD", 1, 0, Q), ("XF", 0, 0, Q), ("XU", 0, 0, A), ("XD", 0, 0, A),
-          ("X", 1, 0, Q), ("X", 2, 0, Q), ("X", 0, 0, Q), ("X", 3, 0, Q)),
-    "U": (("XU", 3, 0, Q), ("F", 3, 0, Q), ("XF", 2, 0, Q), ("F", 2, 0, Q), ("XU", 0, A, B), ("XU", 2, 0, Q),
+    "X": (("X", 1, 0, 512), ("X", 1, 512, 768), ("XU", 1, 0, Q), ("XF", 1, 0, Q), ("XD", 1, 0, Q), ("XF", 0, 0, Q),
+          ("XU", 0, 0, A2), ("XD", 0, 0, A2), ("X", 2, 0, Q), ("X", 0, 0, Q), ("X", 3, 0, Q)),
+    "U": (("XU", 3, 0, Q), ("F", 3, 0, Q), ("XF", 2, 0, Q), ("F", 2, 0, Q), ("XU", 0, A2, B2), ("XU", 2, 0, Q),
           ("U", 1, 0, Q), ("U", 0, 0, Q), ("U", 3, 0, Q), ("U", 2, 0, Q)),
-    "D": (("XF", 3, 0, Q), ("XD", 2, 0, Q), ("D", 3, 0, Q), ("D", 2, 0, Q), ("XD", 0, A, B), ("F", 1, 0, Q),
+    "D": (("D", 3, 0, Q), ("XF", 3, 0, Q), ("XD", 2, 0, Q), ("D", 2, 0, Q), ("XD", 0, A2, B2), ("F", 1, 0, Q),
           ("F", 0, 0, Q), ("XD", 3, 0, Q), ("D", 1, 0, Q), ("D", 0, 0, Q)),
 }
 LINKS = ("X", "U", "D")
@@ -57,8 +59,10 @@
 def arrivals(plan):
     found = {}
     numbers = number(plan)
-    for i in range(10):
+    for i in range(max(len(pieces) for pieces in plan.values())):
         for link in LINKS:
+            if i >= len(plan[link]):
+                continue
             block, quarter, at, size = plan[link][i]
             key = (RENAME[link][block], quarter)
             found.setdefault(key, []).append((numbers[link, i], at, size))
@@ -83,12 +87,12 @@
     rv_hbm,
     pk_hbm,
     pv_hbm,
-    up_ref,
+    up_hbm,
     wq_hbm,
     wk_hbm,
     wv_hbm,
     wo_hbm,
-    out_ref,
+    out_hbm,
     pg_ref,
     blocks,
     wo,
@@ -114,6 +118,7 @@
     p_land_z,
     p_land_h,
     load_sem,
+    store_sem,
     gs_sem,
     gr_sem,
     rs_sem,
@@ -151,6 +156,64 @@
         load(pk_hbm, kv.at[my_slot, :, 0:HEAD]),
         load(pv_hbm, kv.at[my_slot, :, HEAD : 2 * HEAD]),
     ]
+    own_rows = {}
+    for n in (3, 0, 2, 1):
+        cols = pl.ds(n * QUARTER, QUARTER)
+        own_rows[n] = load(up_hbm.at[0, :, cols], blocks.at[0, :, cols])
+    for copy in own_prompt + list(own_rows.values()):
+        copy.wait()
+    pl.semaphore_wait(barrier, len(peers))
+
+    def p_copy(k, src, dst, dev):
+        return pltpu.make_async_remote_copy(
+            src_ref=src, dst_ref=dst, send_sem=ps_sem.at[k], recv_sem=pr_sem.at[k],
+            device_id=dev, device_id_type=MESH,
+        )
+
+    def p_recv(k, dst, dev):
+        p_copy(k, dst, dst, dev).wait_recv()
+
+
+    to_h = p_copy(0, kv.at[my_slot], kv.at[my_slot], dev_h)
+    to_h.start()
+
+    g_number, g_arrive = number(GATHER), arrivals(GATHER)
+    g_sent, g_seen, g_next = [], set(), {link: 0 for link in LINKS}
+
+    def g_copy(k, src_name, dst_name, quarter, at, size, dev):
+        cols = pl.ds(quarter * QUARTER + at, size)
+        return pltpu.make_async_remote_copy(
+            src_ref=blocks.at[POS[src_name], :, cols],
+            dst_ref=blocks.at[POS[dst_name], :, cols],
+            send_sem=gs_sem.at[k], recv_sem=gr_sem.at[k], device_id=dev, device_id_type=MESH,
+        )
+
+    def g_have(name, quarters=(0, 1, 2, 3)):
+        for quarter in quarters:
+            if name == "o" or (name, quarter) in g_seen:
+                continue
+            g_seen.add((name, quarter))
+            for k, at, size in g_arrive[name, quarter]:
+                g_copy(k, name, name, quarter, at, size, device["X"]).wait_recv()
+
+    def g_send(link, count):
+        for _ in range(count):
+            i = g_next[link]
+            g_next[link] = i + 1
+            name, quarter, at, size = GATHER[link][i]
+            g_have(name, (quarter,))
+            copy = g_copy(
+                g_number[link, i], name, RENAME[link][name], quarter, at, size, device[link]
+            )
+            copy.start()
+            g_sent.append(copy)
+
+    for link in LINKS:
+        g_send(link, 1)
+    for _ in range(3):
+        for link in LINKS:
+            g_send(link, 1)
+
     own_q = [
         load(
             q_hbm.at[0, pl.ds(pl.multiple_of(ids[p] * ROWS, ROWS), ROWS)],
@@ -163,62 +226,6 @@
         rows = pl.ds(i * ROWS, ROWS)
         own_keys.append(load(rk_hbm.at[0, rows], kv.at[16 + i, :, 0:HEAD]))
         own_keys.append(load(rv_hbm.at[0, rows], kv.at[16 + i, :, HEAD : 2 * HEAD]))
-
-    position = t * ROWS + lax.broadcasted_iota(jnp.int32, (ROWS, WIDTH), 0)
-    live = position < len_ref[0]
-    blocks[0] = jnp.where(live, up_ref[0], jnp.zeros((), BF))
-
-    pl.semaphore_wait(barrier, len(peers))
-
-    def p_copy(k, src, dst, dev):
-        return pltpu.make_async_remote_copy(
-            src_ref=src, dst_ref=dst, send_sem=ps_sem.at[k], recv_sem=pr_sem.at[k],
-            device_id=dev, device_id_type=MESH,
-        )
-
-    def p_recv(k, dst, dev):
-        p_copy(k, dst, dst, dev).wait_recv()
-
-    for copy in own_prompt:
-        copy.wait()
-    to_h = p_copy(0, kv.at[my_slot], kv.at[my_slot], dev_h)
-    to_h.start()
-
-    g_number, g_arrive = number(GATHER), arrivals(GATHER)
-    g_sent, g_seen, g_next = [], set(), {link: 0 for link in LINKS}
-
-    def g_copy(k, src_name, dst_name, quarter, at, size, dev):
-        cols = pl.ds(quarter * QUARTER + at, size)
-        return pltpu.make_async_remote_copy(
-            src_ref=blocks.at[POS[src_name], :, cols],
-            dst_ref=blocks.at[POS[dst_name], :, cols],
-            send_sem=gs_sem.at[k], recv_sem=gr_sem.at[k], device_id=dev, device_id_type=MESH,
-        )
-
-    def g_have(name, quarters=(0, 1, 2, 3)):
-        for quarter in quarters:
-            if name == "o" or (name, quarter) in g_seen:
-                continue
-            g_seen.add((name, quarter))
-            for k, at, size in g_arrive[name, quarter]:
-                g_copy(k, name, name, quarter, at, size, device["X"]).wait_recv()
-
-    def g_send(link, count):
-        for _ in range(count):
-            i = g_next[link]
-            g_next[link] = i + 1
-            name, quarter, at, size = GATHER[link][i]
-            g_have(name, (quarter,))
-            copy = g_copy(
-                g_number[link, i], name, RENAME[link][name], quarter, at, size, device[link]
-            )
-            copy.start()
-            g_sent.append(copy)
-
-    for _ in range(4):
-        for link in LINKS:
-            g_send(link, 1)
-
     wo_load = load(wo_hbm, wo)
     wc_loads = [
         load(wq_hbm, wc.at[:, 0:640]),
@@ -226,12 +233,20 @@
         load(wv_hbm, wc.at[:, 768:896]),
     ]
     p_recv(0, kv.at[core * 8 + z * 2 + 1 - xh], dev_h)
-    to_z = []
+    to_z, to_s = [], []
     for k in range(3):
         pair = kv.at[pl.ds(core * 8 + z * 2, 2)]
         copy = p_copy(1 + k, pair, pair, dev_z[k])
         copy.start()
         to_z.append(copy)
+
+    def to_other_core(k, at_z):
+        pair = kv.at[pl.ds(core * 8 + at_z * 2, 2)]
+        copy = p_copy(k, pair, pair, dev_s)
+        copy.start()
+        to_s.append(copy)
+
+    to_other_core(4, z)
     dkv[...] = jnp.zeros_like(dkv)
     for copy in own_q:
         copy.wait()
@@ -252,24 +267,21 @@
         vt[c] = values_of(c).astype(F32).T.astype(BF)
         return 0
 
-    lax.fori_loop(4, 6, flip, 0)
-    for k in range(3):
-        p_recv(1 + k, kv.at[pl.ds(core * 8 + ((z + 3 - k) % 4) * 2, 2)], dev_z[k])
-    lane_half = kv.at[pl.ds(core * 8, 8)]
-    to_s = p_copy(4, lane_half, lane_half, dev_s)
-    to_s.start()
-    p_recv(4, kv.at[pl.ds((1 - core) * 8, 8)], dev_s)
-    lax.fori_loop(0, 4, flip, 0)
-
     scaling = 1.0 / math.sqrt(HEAD)
     to_log2 = scaling * math.log2(math.e)
 
-    def softmax(s):
+    def rows_of(s):
         lane = lax.broadcasted_iota(jnp.int32, (1, SUB), 1)
-        row = jnp.where(lane < ROWS, ids[2 * s] * ROWS, ids[2 * s + 1] * ROWS - ROWS) + lane
+        return jnp.where(lane < ROWS, ids[2 * s] * ROWS, ids[2 * s + 1] * ROWS - ROWS) + lane
+
+    no_tops = tuple(jnp.full((1, SUB), -1e30, F32) for _ in range(HEADS))
+
+    def score(s, low, count, tops):
+        row = rows_of(s)
         q_rows = q[s].reshape(LANES, HEAD)
 
-        def first(c, tops):
+        def first(i, tops):
+            c = low + i
             key_at = (c - 4) * CHUNK + lax.broadcasted_iota(jnp.int32, (CHUNK, SUB), 0)
             seen = key_at <= row
             all_heads = dot_nt(keys_of(c), q_rows)
@@ -277,20 +289,21 @@
             for h in range(HEADS):
                 lanes = slice(h * SUB, (h + 1) * SUB)
                 part = jnp.where(seen, all_heads[:, lanes], -1e30)
-                scores[c, :, lanes] = part
+                scores[s % 2, c, :, lanes] = part
                 new.append(jnp.maximum(tops[h], jnp.max(part, axis=0, keepdims=True)))
             return tuple(new)
 
-        tops = lax.fori_loop(
-            0, 6, first, tuple(jnp.full((1, SUB), -1e30, F32) for _ in range(HEADS)), unroll=3
-        )
+        return lax.fori_loop(0, count, first, tops, unroll=min(count, 3))
+
+    def softmax(s, tops):
+        row = rows_of(s)
         out_t[s] = jnp.zeros((HEAD, LANES), F32)
 
         def second(c, sums):
             new = []
             for h in range(HEADS):
                 lanes = slice(h * SUB, (h + 1) * SUB)
-                e = jnp.exp2((scores[c, :, lanes] - tops[h]) * to_log2)
+                e = jnp.exp2((scores[s % 2, c, :, lanes] - tops[h]) * to_log2)
                 prob[s, c, :, lanes] = e.astype(BF)
                 new.append(sums[h] + jnp.sum(e, axis=0, keepdims=True))
             out_t[s] += dot(vt[c], prob[s, c])
@@ -301,7 +314,7 @@
         )
         for h in range(HEADS):
             lanes = slice(h * SUB, (h + 1) * SUB)
-            inverse = 1.0 / sums[h]
+            inverse = jnp.where(row < len_ref[0], 1.0 / sums[h], 0.0)
             out_t[s, :, lanes] = out_t[s, :, lanes] * inverse
             inv[s, h] = jnp.broadcast_to(inverse, (SUB, HEAD)).T
 
@@ -323,7 +336,7 @@
         else:
             go_acc[rows] += part
 
-    def attend(subs):
+    def attend_rows(subs):
         first, count = subs[0], len(subs)
         for s in subs:
             for h in range(HEADS):
@@ -335,6 +348,10 @@
                 )
         wide = count * LANES
         dq_t[:, 0:wide] = jnp.zeros((HEAD, wide), F32)
+
+    def attend_keys(subs, low, high):
+        first, count = subs[0], len(subs)
+        wide = count * LANES
 
         def step(c, _):
             values = values_of(c)
@@ -355,7 +372,9 @@
             dq_t[:, 0:wide] += dot(kt[c], ds[:, 0:wide])
             return 0
 
-        lax.fori_loop(0, 6, step, 0, unroll=3)
+        lax.fori_loop(low, high, step, 0, unroll=min(high - low, 3))
+
+    def attend_done(subs):
         for j, s in enumerate(subs):
             for h in range(HEADS):
                 at = j * LANES + h * SUB
@@ -363,11 +382,29 @@
                     (dq_t[:, at : at + SUB] * scaling).T.astype(BF)
                 )
 
+    def attend(subs):
+        attend_rows(subs)
+        attend_keys(subs, 0, 6)
+        attend_done(subs)
+
+    lax.fori_loop(4, 6, flip, 0)
+    tops = [score(s, 4, 2, no_tops) for s in (0, 1)]
+    for k in range(3):
+        at_z = (z + 3 - k) % 4
+        p_recv(1 + k, kv.at[pl.ds(core * 8 + at_z * 2, 2)], dev_z[k])
+        to_other_core(5 + k, at_z)
+    lax.fori_loop(core * 2, core * 2 + 2, flip, 0)
+    tops = [score(s, core * 2, 2, tops[s]) for s in (0, 1)]
     for link in ("U", "D"):
         g_send(link, 3)
     g_send("X", 2)
-    softmax(0)
-    softmax(1)
+    for k in range(4):
+        at_z = (z + 4 - k) % 4
+        p_recv(4 + k, kv.at[pl.ds((1 - core) * 8 + at_z * 2, 2)], dev_s)
+    lax.fori_loop((1 - core) * 2, (1 - core) * 2 + 2, flip, 0)
+    tops = [score(s, (1 - core) * 2, 2, tops[s]) for s in (0, 1)]
+    softmax(0, tops[0])
+    softmax(1, tops[1])
     wo_load.wait()
     for link in LINKS:
         g_send(link, 2)
@@ -375,10 +412,10 @@
         g_have(name)
     project((0, 1))
     attend((0, 1))
-    softmax(2)
+    softmax(2, score(2, 0, 6, no_tops))
     for link in LINKS:
         g_send(link, 1)
-    softmax(3)
+    softmax(3, score(3, 0, 6, no_tops))
     g_send("X", 1)
     for n, quarter in enumerate((0, 1, 2, 3)):
         g_have("F", (quarter,))
@@ -389,13 +426,13 @@
         g_have("XD", (quarter,))
         g_have("XF", (quarter,))
         project_part(3, quarter, n == 0)
-    attend((3,))
+    attend_rows((3,))
+    attend_keys((3,), 4, 6)
     for copy in g_sent:
         copy.wait_send()
     to_h.wait_send()
-    for copy in to_z:
+    for copy in to_z + to_s:
         copy.wait_send()
-    to_s.wait_send()
 
     dkv_scale = jnp.where(
         lax.broadcasted_iota(jnp.int32, (1, 1, 2 * HEAD), 2) < HEAD, scaling, 1.0
@@ -439,90 +476,124 @@
             copy.start()
             r_sent.append(copy)
 
-    def term(half, quarter):
-        rows = slice(half * 256, half * 256 + 256)
-        for k in range(5):
+    def term(low, high, quarter, parts=(0, 1, 2, 3, 4)):
+        rows = slice(low * ROWS, high * ROWS)
+        for k in parts:
             start = quarter * QUARTER + k * 256
             value = dot_nt(grads[rows, :], wc[start : start + 256, :]).astype(BF)
-            blocks[half * 4 : half * 4 + 4, :, start : start + 256] = value.reshape(4, ROWS, 256)
-
-    term(1, 1)
-    r_send("X", 3)
-    term(1, 3)
+            blocks[low:high, :, start : start + 256] = value.reshape(high - low, ROWS, 256)
+
+    term(0, 6, 1, (0, 1))
+    r_send("X", 1)
+    term(0, 6, 1, (2, 3, 4))
+    r_send("X", 2)
+    term(0, 6, 3)
     r_send("U", 2)
     r_send("D", 1)
-    term(1, 2)
-    r_send("U", 2)
+    attend_keys((3,), 0, 4)
+    attend_done((3,))
+    term(6, 8, 3)
     r_send("D", 1)
-    term(1, 0)
+    term(6, 8, 2)
+    r_send("U", 1)
+    r_send("D", 1)
+    term(6, 8, 1)
+    r_send("X", 2)
+    term(0, 6, 2)
+    r_send("U", 1)
+    r_send("D", 1)
+    term(6, 8, 0)
+    term(0, 6, 0)
     r_send("X", 3)
     r_send("U", 1)
+    r_send("D", 1)
     p_send[...] = (dkv[pl.ds((1 - core) * 8, 8)] * dkv_scale).astype(BF)
-    ps = p_copy(5, p_send, p_land, dev_s)
+    ps = p_copy(8, p_send, p_land, dev_s)
     ps.start()
-    term(0, 3)
     r_send("D", 1)
-    term(0, 2)
-    r_send("D", 2)
-    term(0, 1)
-    r_send("X", 1)
-    r_send("D", 1)
-    term(0, 0)
+    r_send("U", 2)
 
     ps.wait_send()
-    p_recv(5, p_land, dev_s)
+    p_recv(8, p_land, dev_s)
     mine = pl.ds(core * 8, 8)
     dkv[mine] = dkv[mine] * dkv_scale + p_land[...].astype(F32)
     p_send[...] = dkv[mine].astype(BF)
     z_copies = []
     for k in range(3):
         peer_z = (z + 1 + k) % 4
-        copy = p_copy(6 + k, p_send.at[pl.ds(peer_z * 2, 2)], p_land_z.at[k], dev_z[k])
+        copy = p_copy(9 + k, p_send.at[pl.ds(peer_z * 2, 2)], p_land_z.at[k], dev_z[k])
         copy.start()
         z_copies.append(copy)
 
-    r_send("U", 2)
+    r_send("D", 2)
+    r_send("U", 3)
 
     for k in range(3):
         z_copies[k].wait_send()
-        p_recv(6 + k, p_land_z.at[k], dev_z[k])
+        p_recv(9 + k, p_land_z.at[k], dev_z[k])
     pair_at = core * 8 + z * 2
     both = dkv[pl.ds(pair_at, 2)]
     for k in range(3):
         both = both + p_land_z[k].astype(F32)
     dkv[pl.ds(pair_at, 2)] = both
     p_send[0] = dkv[pair_at + 1 - xh].astype(BF)
-    ph = p_copy(9, p_send.at[0], p_land_h, dev_h)
+    ph = p_copy(12, p_send.at[0], p_land_h, dev_h)
     ph.start()
 
-    r_send("D", 2)
-    r_send("U", 3)
-    p_recv(9, p_land_h, dev_h)
-    pg_ref[...] = dkv[pair_at + xh] + p_land_h[...].astype(F32)
     r_send("X", 2)
     r_send("D", 2)
     r_send("X", 1)
-    ph.wait_send()
-
-    for quarter in (0, 1, 2, 3):
-        cols = slice(quarter * QUARTER, (quarter + 1) * QUARTER)
+    p_recv(12, p_land_h, dev_h)
+    pg_ref[...] = dkv[pair_at + xh] + p_land_h[...].astype(F32)
+    to_h_sent = [ph]
+
+    stores = []
+    for n, quarter in enumerate((1, 3, 0, 2)):
+        cols = pl.ds(quarter * QUARTER, QUARTER)
         total = blocks[0, :, cols].astype(F32)
+        strips = []
         for k, at, size in r_arrive["o", quarter]:
             r_wait(k, size)
-            total = total + landed[k].astype(F32)
-        out_ref[0, :, cols] = total.astype(BF)
-    for copy in r_sent:
+            if size == QUARTER:
+                total = total + landed[k].astype(F32)
+            else:
+                strips.append((at, landed[k, :, 0:size].astype(F32)))
+        if strips:
+            strips.sort(key=lambda strip: strip[0])
+            total = total + jnp.concatenate([strip[1] for strip in strips], axis=1)
+        blocks[0, :, cols] = total.astype(BF)
+        copy = pltpu.make_async_copy(blocks.at[0, :, cols], out_hbm.at[0, :, cols], store_sem.at[n])
+        copy.start()
+        stores.append(copy)
+    for copy in r_sent + to_h_sent:
         copy.wait_send()
-
-
-def split_kernel(rows_ref, both_ref, out_ref, key_ref, value_ref):
-    out_ref[...] = rows_ref[...]
-    key_ref[...] = both_ref[:, 0:HEAD]
-    value_ref[...] = both_ref[:, HEAD : 2 * HEAD]
+    for copy in stores:
+        copy.wait()
+
+
+def split_kernel(rows_hbm, both_hbm, out_hbm, key_hbm, value_hbm, rows, both, in_sem, out_sem):
+    parts = []
+    for n in range(4):
+        at = pl.ds(n * 16, 16)
+        parts.append((rows_hbm.at[0, at], rows.at[at], ((rows.at[at], out_hbm.at[0, at]),)))
+    key, value = both.at[:, 0:HEAD], both.at[:, HEAD : 2 * HEAD]
+    parts.append((both_hbm, both, ((key, key_hbm), (value, value_hbm))))
+    reads = [pltpu.make_async_copy(p[0], p[1], in_sem.at[n]) for n, p in enumerate(parts)]
+    for copy in reads:
+        copy.start()
+    writes = []
+    for read, part in zip(reads, parts):
+        read.wait()
+        for src, dst in part[2]:
+            copy = pltpu.make_async_copy(src, dst, out_sem.at[len(writes)])
+            copy.start()
+            writes.append(copy)
+    for copy in writes:
+        copy.wait()
 
 
 def split(input_grad, prompt_grads):
-    vmem = pl.BlockSpec(memory_space=pltpu.VMEM)
+    hbm = pl.BlockSpec(memory_space=pl.ANY)
     return pl.pallas_call(
         split_kernel,
         out_shape=(
@@ -530,8 +601,14 @@
             jax.ShapeDtypeStruct((ROWS, HEAD), F32),
             jax.ShapeDtypeStruct((ROWS, HEAD), F32),
         ),
-        in_specs=[vmem, vmem],
-        out_specs=(vmem, vmem, vmem),
+        in_specs=[hbm, hbm],
+        out_specs=(hbm, hbm, hbm),
+        scratch_shapes=[
+            pltpu.VMEM((ROWS, WIDTH), BF),
+            pltpu.VMEM((ROWS, 2 * HEAD), F32),
+            pltpu.SemaphoreType.DMA((5,)),
+            pltpu.SemaphoreType.DMA((6,)),
+        ],
     )(input_grad, prompt_grads)
 
 
@@ -558,8 +635,8 @@
             jax.ShapeDtypeStruct((1, ROWS, WIDTH), BF),
             jax.ShapeDtypeStruct((ROWS, 2 * HEAD), F32),
         ),
-        in_specs=[smem, hbm, hbm, hbm, hbm, hbm, vmem, hbm, hbm, hbm, hbm],
-        out_specs=(vmem, vmem),
+        in_specs=[smem] + [hbm] * 10,
+        out_specs=(hbm, vmem),
         scratch_shapes=[
             pltpu.VMEM((8, ROWS, WIDTH), BF),
             pltpu.VMEM((HEADS * HEAD, WIDTH), BF),
@@ -568,7 +645,7 @@
             pltpu.VMEM((24, ROWS, 2 * HEAD), BF),
             pltpu.VMEM((6, HEAD, CHUNK), BF),
             pltpu.VMEM((6, HEAD, CHUNK), BF),
-            pltpu.VMEM((6, CHUNK, LANES), F32),
+            pltpu.VMEM((2, 6, CHUNK, LANES), F32),
             pltpu.VMEM((4, 6, CHUNK, LANES), BF),
             pltpu.VMEM((4, HEAD, LANES), F32),
             pltpu.VMEM((4 * SUB, HEADS * HEAD), F32),
@@ -579,18 +656,19 @@
             pltpu.VMEM((HEAD, 2 * LANES), F32),
             pltpu.VMEM((24, ROWS, 2 * HEAD), F32),
             pltpu.VMEM((8 * ROWS, 896), BF),
-            pltpu.VMEM((30, ROWS, QUARTER), BF),
+            pltpu.VMEM((31, ROWS, QUARTER), BF),
             pltpu.VMEM((8, ROWS, 2 * HEAD), BF),
             pltpu.VMEM((8, ROWS, 2 * HEAD), BF),
             pltpu.VMEM((3, 2, ROWS, 2 * HEAD), BF),
             pltpu.VMEM((ROWS, 2 * HEAD), BF),
-            dma((32,)),
+            dma((36,)),
+            dma((4,)),
             dma((30,)),
             dma((30,)),
-            dma((30,)),
-            dma((30,)),
-            dma((10,)),
-            dma((10,)),
+            dma((31,)),
+            dma((31,)),
+            dma((13,)),
+            dma((13,)),
         ],
         compiler_params=pltpu.CompilerParams(
             collective_id=0, has_side_effects=True, vmem_limit_bytes=62 * 1024 * 1024

time: 87.8 us -> 86.5 us (0.985)
  Pallas kernels: 85.3 us -> 83.8 us
    pallas_call x1, Pallas kernels: 83.3 us -> 81.8 us  [body(): pl.pallas_call(kernel, out_shape=(jax.ShapeDtypeStruct((1, ROWS, WIDTH),...]
where the time goes in v4:
time: 86.5 us; the launch traced here: 85.2 us
  Pallas kernels  83.8 us (97%)
  between operations  1.45 us (2%)
    pallas_call x1, Pallas kernels, body(): pl.pallas_call(kernel, out_shape=(jax.ShapeDtypeStruct((1, ROWS, WIDTH),...  81.8 us
    pallas_call x1, Pallas kernels, split(): pl.pallas_call(split_kernel, out_shape=(jax.ShapeDtypeStruct((1, ROWS, WI...  1.93 us

profile of v4, /device:TPU:1, one launch (start us, length us, event | category | flops | bytes accessed | tf_op | source)
XLA Modules:
  0.0 85.2 jit_solution(11005342044091718954)
XLA Ops:
  1.3 81.8 %shard_map.130 = (bf16[1,64,5120]{2,1,0:T(8,128)(2,1)}, f32[64,256]{1,0:T(8,128)}) custom-call(s32[1]{0:T(128)S(6)} %copy.14.len_ref, bf16[1,512,640]{2,1,0:T(8,128)(2,1)} %q_hbm.1, bf16[1,512,128]{2,1,0:T(8,128)(2,1)} %rk_hbm.1, bf16[1,512,128]{2,1,0:T(8,128)(2,1)} %rv_hbm.1, bf16[64,128]{1,0:T(8,128)(2,1)} %pk_hbm.1, bf16[64,128]{1,0:T(8,128)(2,1)} %pv_hbm.1, ...), custom_call_target="tpu_custom_call" | custom-call | flops 17999998976 | bytes 20000000 | tf_op jit(solution)/shard_map/pallas_call | solution.py:632
  83.1 1.9 %shard_map.131 = (bf16[1,64,5120]{2,1,0:T(8,128)(2,1)}, f32[64,128]{1,0:T(8,128)}, f32[64,128]{1,0:T(8,128)}) custom-call(bf16[1,64,5120]{2,1,0:T(8,128)(2,1)} %get-tuple-element.5.rows_hbm, f32[64,256]{1,0:T(8,128)} %get-tuple-element.6.both_hbm), custom_call_target="tpu_custom_call" | custom-call | tf_op jit(solution)/shard_map/pallas_call | solution.py:597
